TPU v7x, 32 devices: a whole 2x2x4 slice. The times are simulated.
32 devices in a mesh: row: 8 (over z, x), col: 4 (over y, core).
Axes of the slice: x: 2, y: 2, z: 4, core: 2. Of those that a mesh axis runs over, the one named last changes fastest.
Arguments:
- start_vectors: float32 [64, 16384], P(None, ('row', 'col')), may hold values from -6 to 6
- scaling: float32 [16384], P(('row', 'col')), may hold values from 0.25 to 1.75
- block_values: bfloat16 [8, 4, 128, 128, 128], P('row', 'col'), may hold values from -0.046875 to 0.046875
- block_places: int32 [8, 4, 2, 128], P('row', 'col'), may hold values from 0 to 31, as said below
- block_counts: int32 [8, 4], P('row', 'col'), may hold values from 16 to 128, as said below
Outputs:
- filtered: float32 [64, 16384], P(None, ('row', 'col'))
Inputs may be any that keep to these rules, and one draw needn't show every extreme that they name: `block_places`: within each device's 128 slots the positions (block row, block column) are distinct; entry 0 is the local block row (below 16), entry 1 the local block column (below 32). Slots at or after the device's count are not part of the matrix. `block_counts`: some device has all 128 slots live.
All inputs are finite; a program needn't handle non-finite values.
Results may differ from a plain program's by a relative error of at most 0.0038.
Values may be sent and summed in bfloat16 or wider, within the bound.
No kernel may reach another device: no remote copies, remote signals or barrier semaphores. Data moves between devices by JAX's collectives and lax.ppermute only.
A program may use at most 128 MiB of HBM per device.

v0:
```python
import functools

import jax
import jax.numpy as jnp
from jax import lax
from jax.experimental import pallas as pl
from jax.experimental.pallas import tpu as pltpu
from jax.sharding import PartitionSpec as P

STEPS = 3

center_shift = 0.5
half_width = 3.0

UNROLL = 64
PACK = 4
VMEM_LIMIT = 16 * 1024 * 1024
AXES = ("row", "col")
PAD = 8


class Layout:
    def __init__(self, rows, cols):
        self.rows, self.cols = rows, cols
        self.chips = cols // 2
        self.fast = 2
        self.slow = rows // 2
        self.group = self.slow // self.chips
        assert self.group * self.chips * self.fast == rows

    def device(self, slow, fast, chip, core):
        return (slow * self.fast + fast) * self.cols + chip * 2 + core

    def home(self, chunk):
        chip, k = chunk // self.rows, chunk % self.rows
        e, f, t = k % self.chips, (k // self.chips) % self.fast, k // (self.chips * self.fast)
        return (chip ^ e) * self.group + t, f, chip

    def moves_home(self, swap):
        pairs = []
        for chunk in range(self.rows * self.chips):
            row, chip = chunk // self.chips, chunk % self.chips
            for core in range(2):
                source = row * self.cols + chip * 2 + core
                pairs.append((source, self.device(*self.home(chunk), core ^ swap)))
        return pairs

    def moves_slow(self, d, side=0):
        return [
            (self.device(s, f, c, q), self.device(s ^ d, f ^ side, c, q))
            for s in range(self.slow) for f in range(self.fast)
            for c in range(self.chips) for q in range(2)
        ]

    def moves_fast(self):
        return self.moves_slow(0, 1)

    def moves_chip(self, d, swap=0):
        return [
            (self.device(s, f, c, q), self.device(s, f, c ^ d, q ^ swap))
            for s in range(self.slow) for f in range(self.fast)
            for c in range(self.chips) for q in range(2)
        ]

    def moves_core(self):
        return [(i, i ^ 1) for i in range(self.rows * self.cols)]


def turned(pairs):
    return [(b, a) for a, b in pairs]


def live_groups(meta_ref, cap, which):
    return jnp.maximum((meta_ref[8 * cap + which] + (UNROLL - 1)) // UNROLL, 1)


def product_kernel(transpose, cap, n_out, after, meta_in, vecs_in, *refs):
    slab_refs, refs = refs[:2], refs[2 + after:]
    outs, refs = refs[:n_out], refs[n_out:]
    meta_ref, vecs_ref, slabs, acc, slab_sem, in_sem = refs
    base = 0 if transpose else 4 * cap

    def slab_copy(which, g):
        span = pl.ds(g * UNROLL, UNROLL)
        to = pl.ds(which * cap + g * UNROLL, UNROLL)
        sem = slab_sem.at[which * (cap // UNROLL) + g]
        return pltpu.make_async_copy(slab_refs[which].at[span], slabs.at[to], sem)

    def start_slab(which, g, carry):
        slab_copy(which, g).start()
        return carry

    meta_copy = pltpu.make_async_copy(meta_in, meta_ref, in_sem.at[0])
    vecs_copy = pltpu.make_async_copy(vecs_in, vecs_ref, in_sem.at[1])
    meta_copy.start()
    slab_copy(0, 0).start()
    vecs_copy.start()
    slab_copy(1, 0).start()
    acc[...] = jnp.zeros_like(acc)
    meta_copy.wait()
    groups = [live_groups(meta_ref, cap, which) for which in range(2)]
    for which in range(2):
        lax.fori_loop(1, groups[which], functools.partial(start_slab, which), 0)
    vecs_copy.wait()
    vec_count, block_len = vecs_ref.shape[1:]
    zero = jnp.zeros((vec_count, block_len), jnp.bfloat16)

    def body(which, g, carry):
        slab_copy(which, g).wait()
        start = which * cap + g * UNROLL
        products = []
        for u in range(0, UNROLL, PACK):
            v = [vecs_ref[meta_ref[base + start + u + k]] for k in range(PACK)]
            m = [slabs[start + u + k] for k in range(PACK)]
            left = jnp.concatenate([
                jnp.concatenate([v[0], zero, v[2], zero], axis=0),
                jnp.concatenate([zero, v[1], zero, v[3]], axis=0),
            ], axis=1)
            if transpose:
                halves = [jnp.concatenate(m[:2], axis=0), jnp.concatenate(m[2:], axis=0)]
                right, dims = jnp.concatenate(halves, axis=1), (((1,), (0,)), ((), ()))
            else:
                halves = [jnp.concatenate(m[:2], axis=1), jnp.concatenate(m[2:], axis=1)]
                right, dims = jnp.concatenate(halves, axis=0), (((1,), (1,)), ((), ()))
            products.append(
                lax.dot_general(left, right, dims, preferred_element_type=jnp.float32)
            )
        for u in range(UNROLL):
            k = u % PACK
            rows = slice(k * vec_count, (k + 1) * vec_count)
            lanes = slice((k // 2) * block_len, (k // 2 + 1) * block_len)
            acc[meta_ref[base + 2 * cap + start + u]] += products[u // PACK][rows, lanes]
        return carry

    for which in range(2):
        lax.fori_loop(0, groups[which], functools.partial(body, which), 0)
    size = outs[0].shape[0]
    for k, out in enumerate(outs):
        out[...] = acc[k * size:(k + 1) * size].astype(out.dtype)


def products(meta, slabs, vecs, out_dtypes, out_blocks, transpose, after=()):
    cap, block_len, _ = slabs[0].shape
    vec_count = vecs.shape[1]
    n_out = len(out_dtypes)
    total_out = out_blocks * n_out
    anywhere = pl.BlockSpec(memory_space=pl.ANY)
    vmem = pl.BlockSpec(memory_space=pltpu.VMEM)
    out_shape = [
        jax.ShapeDtypeStruct((out_blocks, vec_count, block_len), dtype) for dtype in out_dtypes
    ]
    return pl.pallas_call(
        functools.partial(product_kernel, transpose, cap, n_out, len(after)),
        in_specs=[anywhere] * (4 + len(after)),
        out_specs=[vmem] * n_out,
        out_shape=out_shape,
        scratch_shapes=[
            pltpu.SMEM(meta.shape, jnp.int32),
            pltpu.VMEM(vecs.shape, jnp.bfloat16),
            pltpu.VMEM((2 * cap, block_len, block_len), jnp.bfloat16),
            pltpu.VMEM((total_out + 1, vec_count, block_len), jnp.float32),
            pltpu.SemaphoreType.DMA((2 * cap // UNROLL,)),
            pltpu.SemaphoreType.DMA((2,)),
        ],
        compiler_params=pltpu.CompilerParams(vmem_limit_bytes=VMEM_LIMIT),
        cost_estimate=pl.CostEstimate(
            flops=4 * cap * vec_count * block_len * block_len,
            bytes_accessed=2 * vec_count * block_len * (vecs.shape[0] + total_out),
            transcendentals=0,
        ),
        name="transposed" if transpose else "direct",
    )(meta, vecs, *slabs, *after)


def per_device(start_vectors, scaling, block_values, block_places, block_counts):
    at = Layout(lax.axis_size("row"), lax.axis_size("col"))
    cap = block_values.shape[2]
    block_len = block_values.shape[-1]
    half = start_vectors.shape[0] // 2
    part = start_vectors.shape[1] // block_len
    per_chunk = 2 * part
    row_index = lax.axis_index("row").astype(jnp.int32)
    col_index = lax.axis_index("col").astype(jnp.int32)
    slow, fast = row_index // at.fast, row_index % at.fast
    chip, core = col_index // 2, col_index % 2
    root = slow // at.group
    is_root = chip == root
    def send(x, pairs):
        return lax.ppermute(x, AXES, pairs)

    slabs = block_values.reshape(cap, block_len, block_len)
    slots = jnp.concatenate([block_places.reshape(2 * cap), block_counts.reshape(1)])
    other_slabs = send(slabs, at.moves_core())

    halves = start_vectors.reshape(2, half, part, block_len).transpose(0, 2, 1, 3)
    scale_rows = jnp.broadcast_to(
        scaling.reshape(1, part, 1, block_len), (2, part, PAD, block_len)
    )
    halves = jnp.concatenate([halves, scale_rows], axis=2)
    packed = [
        jnp.where(core == swap, halves[0], halves[1]) for swap in range(2)
    ]
    pieces = [
        jnp.concatenate([
            packed[swap] if (d, swap) == (0, 0) else send(packed[swap], at.moves_chip(d, swap))
            for swap in range(2)
        ], axis=0)
        for d in range(at.chips)
    ]
    n_kept = at.chips * per_chunk

    def chunk_of(x, e):
        return x[e * per_chunk:(e + 1) * per_chunk]

    def pick(index, choices):
        x = choices[0]
        for d in range(1, len(choices)):
            x = jnp.where(index == d, choices[d], x)
        return x

    row_state = jnp.concatenate([pick(chip ^ e, pieces) for e in range(at.chips)], axis=0)

    other_slots = send(slots, at.moves_core())
    n_col = at.rows * per_chunk
    n_row = at.chips * per_chunk
    lists = []
    for which, held in enumerate((slots, other_slots)):
        row_block, col_block = held[:cap], held[cap:2 * cap]
        live = jnp.arange(cap, dtype=jnp.int32) < held[2 * cap]

        def inside(block):
            return ((block // part) ^ core) * part + block % part

        e = row_block // per_chunk
        row_at = e * per_chunk + inside(row_block % per_chunk)
        block = (core ^ which) * (n_col // 2) + col_block
        k = block // per_chunk
        e, f, t = k % at.chips, (k // at.chips) % at.fast, k // (at.chips * at.fast)
        d = slow ^ ((chip ^ e) * at.group + t)
        place = (d % at.group) * at.chips + d // at.group
        col_at = ((fast ^ f) * at.slow + place) * per_chunk + inside(block % per_chunk)
        lists.append((
            row_at, jnp.where(live, col_at, n_col), col_at, jnp.where(live, row_at, n_row)
        ))
    meta = jnp.concatenate(
        [jnp.concatenate([mine, theirs]) for mine, theirs in zip(*lists)]
        + [slots[2 * cap:], other_slots[2 * cap:], jnp.zeros(126, jnp.int32)]
    )

    row_state, meta, other_slabs = lax.optimization_barrier((row_state, meta, other_slabs))
    both = (slabs, other_slabs)

    def across(x):
        return [send(x, at.moves_slow(d * at.group)) for d in range(1, at.chips)]

    def kept_of(x, got):
        got = [
            jnp.concatenate([chunk_of(y, k ^ d) for k in range(at.chips)], axis=0)
            for d, y in enumerate(got, 1)
        ]
        return pick(chip ^ root, [x] + got)

    row_now, row_scale = row_state[:, :half], row_state[:, half:half + 1]
    row_tile = (row_scale * row_now).astype(jnp.bfloat16)
    tiles_across = across(row_tile)
    row_tile, row_state = lax.optimization_barrier((row_tile, row_state))
    row_now, row_scale = row_state[:, :half], row_state[:, half:half + 1]
    high = lax.optimization_barrier(row_scale.astype(jnp.bfloat16))
    low = lax.optimization_barrier(
        (row_scale - high.astype(jnp.float32)).astype(jnp.bfloat16)
    )

    def joined(high, low):
        return high.astype(jnp.float32) + low.astype(jnp.float32)

    row_rest = (
        row_now - row_tile.astype(jnp.float32) / joined(high, low)
    ).astype(jnp.bfloat16)
    row_rest = jnp.concatenate(
        [row_rest] + [jnp.broadcast_to(x, (n_kept, PAD, block_len)) for x in (high, low)],
        axis=1,
    )

    before = None
    for iterate in range(STEPS):
        first, last = iterate == 0, iterate == STEPS - 1
        if not first:
            row_tile = pick(
                chip ^ root,
                [own] + [send(own, at.moves_chip(d)) for d in range(1, at.chips)],
            )
        dtypes = (jnp.float32,) * at.group + (jnp.bfloat16,) * at.group
        if not first:
            near = [own] + [send(own, at.moves_slow(g)) for g in range(1, at.group)]
            far = [send(own, at.moves_slow(g, 1)) for g in range(at.group)]
        sums = products(meta, both, row_tile, dtypes, n_kept, True)
        near_sums, far_sums = list(sums[:at.group]), list(sums[at.group:])
        from_fast = [send(x, at.moves_fast()) for x in far_sums[::-1]][::-1]
        if first:
            tiles_across, far_sums = lax.optimization_barrier((tiles_across, far_sums))
            own = kept_of(row_tile, tiles_across)
            near = [own] + [send(own, at.moves_slow(g)) for g in range(1, at.group)]
            far = [send(own, at.moves_slow(g, 1)) for g in range(at.group)]
            row_rest, near = lax.optimization_barrier((row_rest, near))
            rests_across = across(row_rest)
        (row_sum,) = products(
            meta, both, jnp.concatenate(near + far, axis=0), (jnp.bfloat16,), n_row, False,
            after=far_sums,
        )
        if first:
            from_fast[-1], row_sum, rests_across = lax.optimization_barrier(
                (from_fast[-1], row_sum, rests_across)
            )
            scales = [
                joined(x[:, half:half + 1], x[:, half + PAD:half + PAD + 1])
                for x in rests_across
            ]
            scale = kept_of(row_scale, scales)
            now = kept_of(row_now, [
                tile.astype(jnp.float32) / factor + rest[:, :half].astype(jnp.float32)
                for tile, factor, rest in zip(tiles_across, scales, rests_across)
            ])
        from_row = [row_sum] + [
            send(row_sum, at.moves_chip(d)) for d in range(1, at.chips)
        ]
        sums = [x + y.astype(jnp.float32) for x, y in zip(near_sums, from_fast)]
        total = sums[0]
        for g in range(1, at.group):
            total = total + send(
                sums[g].astype(jnp.bfloat16), at.moves_slow(g)
            ).astype(jnp.float32)
        for x in from_row:
            total = total + jnp.where(is_root, x, jnp.zeros_like(x)).astype(jnp.float32)
        message = total.astype(jnp.bfloat16)
        if last:
            total, now, scale = chunk_of(total, 0), chunk_of(now, 0), chunk_of(scale, 0)
            before = chunk_of(before, 0)
        applied = total
        for e in range(1, at.chips):
            if last:
                got = send(chunk_of(message, e), at.moves_slow(e * at.group))
            else:
                got = send(message, at.moves_slow(e * at.group))
                got = jnp.concatenate([chunk_of(got, k ^ e) for k in range(at.chips)], axis=0)
            applied = applied + got.astype(jnp.float32)
        mapped = scale * applied - center_shift * now
        if first:
            updated = mapped / half_width
        else:
            updated = 2.0 / half_width * mapped - before
        before = now
        now = updated
        if not last:
            own = (scale * now).astype(jnp.bfloat16)
    back = [
        send(now[swap * part:(swap + 1) * part], turned(at.moves_home(swap)))
        for swap in range(2)
    ]
    result = jnp.stack([jnp.where(core == k, back[0], back[1]) for k in range(2)])
    return result.transpose(0, 2, 1, 3).reshape(start_vectors.shape)


def solution(mesh):
    in_specs = (
        P(None, ("row", "col")),
        P(("row", "col")),
        P("row", "col", None, None, None),
        P("row", "col", None, None),
        P("row", "col"),
    )
    out_specs = P(None, ("row", "col"))
    return jax.shard_map(
        per_device, mesh=mesh, in_specs=in_specs, out_specs=out_specs, check_vma=False
    )
```

profile of v0, /device:TPU:5, one launch (start us, length us, event | category | flops | bytes accessed | tf_op | source)
XLA Modules:
  0.0 115.3 jit_solution(16588322021197244210)
XLA Ops:
  0.0 0.7 collective-permute-start.4
  0.7 0.9 reshape.25
  1.6 0.7 broadcast_in_dim.34
  3.2 0.7 pad_add_fusion
  3.8 0.4 collective-permute-start.3
  4.3 1.4 %collective-permute-start = (f32[4,40,128]{2,1,0:T(8,128)S(1)}, f32[4,40,128]{2,1,0:T(8,128)S(1)}, u32[]{:S(2)}, u32[]{:S(2)}) collective-permute-start(f32[4,40,128]{2,1,0:T(8,128)S(1)} %get-tuple-element.78), channel_id=1, source_target_pairs={{0,2},{1,3},{2,0},{3,1},{4,6},{5,7},{6,4},{7,5},{8,10},{9,11},{10,... | collective-permute-start | bytes 245768 | tf_op jit(solution)/shard_map/ppermute | solution.py:189
  5.7 0.8 compare_select_fusion.37
  6.5 1.1 collective-permute-done.3
  7.6 0.5 slice.106
  8.1 0.7 compare_select_fusion.35
  8.8 0.7 concatenate.50.meta_in
  9.7 2.4 %collective-permute-start.6 = (bf16[16,32,128]{2,1,0:T(8,128)(2,1)S(1)}, bf16[16,32,128]{2,1,0:T(8,128)(2,1)S(1)}, u32[]{:S(2)}, u32[]{:S(2)}) collective-permute-start(bf16[16,32,128]{2,1,0:T(8,128)(2,1)S(1)} %multiply_convert_fusion.2.vecs_in), channel_id=1, source_target_pairs={{0,16},{1,17},{2,18},{3,19},{4,20},{5,21},{6,22},{7,23},{8,24},{9,... | collective-permute-start | bytes 393224 | tf_op jit(solution)/shard_map/ppermute | solution.py:189
  12.1 2.2 %copy-done = bf16[1,1,128,128,128]{4,3,2,1,0:T(8,128)(2,1)S(1)} copy-done((bf16[1,1,128,128,128]{4,3,2,1,0:T(8,128)(2,1)S(1)}, bf16[1,1,128,128,128]{4,3,2,1,0:T(8,128)(2,1)}, u32[]{:S(2)}) %copy-start) | copy-done | bytes 4194328
  14.3 2.7 %transposed.3 = (f32[16,32,128]{2,1,0:T(8,128)S(1)}, f32[16,32,128]{2,1,0:T(8,128)S(1)}, bf16[16,32,128]{2,1,0:T(8,128)(2,1)S(1)}, bf16[16,32,128]{2,1,0:T(8,128)(2,1)S(1)}) custom-call(s32[1152]{0:T(1024)S(1)} %concatenate.50.meta_in, bf16[16,32,128]{2,1,0:T(8,128)(2,1)S(1)} %multiply_convert_fusion.2.vecs_in, bf16[128,128,128]{2,1,0:T(8,128)(2,1)S(1)} %bitcast.67, ...), custom_call_target="tpu_custom_call" | custom-call | flops 268435456 | bytes 655360 | tf_op jit(solution)/shard_map/transposed/pallas_call | solution.py:152
  17.0 1.2 %collective-permute-done.6 = bf16[16,32,128]{2,1,0:T(8,128)(2,1)S(1)} collective-permute-done((bf16[16,32,128]{2,1,0:T(8,128)(2,1)S(1)}, bf16[16,32,128]{2,1,0:T(8,128)(2,1)S(1)}, u32[]{:S(2)}, u32[]{:S(2)}) %collective-permute-start.6) | collective-permute-done | bytes 131104 | tf_op jit(solution)/shard_map/ppermute | solution.py:189
  18.2 1.2 %collective-permute-start.7 = (bf16[16,32,128]{2,1,0:T(8,128)(2,1)S(1)}, bf16[16,32,128]{2,1,0:T(8,128)(2,1)S(1)}, u32[]{:S(2)}, u32[]{:S(2)}) collective-permute-start(bf16[16,32,128]{2,1,0:T(8,128)(2,1)S(1)} %maximum_select_fusion.1), channel_id=1, source_target_pairs={{0,8},{1,9},{2,10},{3,11},{4,12},{5,13},{6,14},{7,15},{8,0},{9,1},... | collective-permute-start | bytes 393224 | tf_op jit(solution)/shard_map/ppermute | solution.py:189
  19.5 1.3 %collective-permute-start.9 = (bf16[16,32,128]{2,1,0:T(8,128)(2,1)S(1)}, bf16[16,32,128]{2,1,0:T(8,128)(2,1)S(1)}, u32[]{:S(2)}, u32[]{:S(2)}) collective-permute-start(bf16[16,32,128]{2,1,0:T(8,128)(2,1)S(1)} %maximum_select_fusion.1), channel_id=1, source_target_pairs={{0,12},{1,13},{2,14},{3,15},{4,8},{5,9},{6,10},{7,11},{8,4},{9,5},... | collective-permute-start | bytes 393224 | tf_op jit(solution)/shard_map/ppermute | solution.py:189
  20.8 0.3 collective-permute-start.8
  21.1 1.0 collective-permute-done.7
  22.1 3.8 %collective-permute-start.10 = (bf16[16,48,128]{2,1,0:T(8,128)(2,1)S(1)}, bf16[16,48,128]{2,1,0:T(8,128)(2,1)S(1)}, u32[]{:S(2)}, u32[]{:S(2)}) collective-permute-start(bf16[16,48,128]{2,1,0:T(8,128)(2,1)S(1)} %pad_maximum_fusion.4), channel_id=1, source_target_pairs={{0,16},{1,17},{2,18},{3,19},{4,20},{5,21},{6,22},{7,23},{8,24},{9,... | collective-permute-start | bytes 589832 | tf_op jit(solution)/shard_map/ppermute | solution.py:189
  26.0 1.2 %collective-permute-start.5 = (bf16[16,32,128]{2,1,0:T(8,128)(2,1)S(1)}, bf16[16,32,128]{2,1,0:T(8,128)(2,1)S(1)}, u32[]{:S(2)}, u32[]{:S(2)}) collective-permute-start(bf16[16,32,128]{2,1,0:T(8,128)(2,1)S(1)} %get-tuple-element.42.refs_3_), channel_id=1, source_target_pairs={{0,4},{1,5},{2,6},{3,7},{4,0},{5,1},{6,2},{7,3},{8,12},{9,13},{10,... | collective-permute-start | bytes 393224 | tf_op jit(solution)/shard_map/ppermute | solution.py:189
  27.2 0.3 collective-permute-start.11
  27.4 0.4 collective-permute-done.8
  27.9 2.2 %copy-done.1 = bf16[1,1,128,128,128]{4,3,2,1,0:T(8,128)(2,1)S(1)} copy-done((bf16[1,1,128,128,128]{4,3,2,1,0:T(8,128)(2,1)S(1)}, bf16[1,1,128,128,128]{4,3,2,1,0:T(8,128)(2,1)}, u32[]{:S(2)}) %copy-start.1) | copy-done | bytes 4194328
  30.1 2.7 %direct.3 = bf16[16,32,128]{2,1,0:T(8,128)(2,1)S(1)} custom-call(s32[1152]{0:T(1024)S(1)} %concatenate.50.meta_in, bf16[64,32,128]{2,1,0:T(8,128)(2,1)S(1)} %pad_maximum_fusion.vecs_in, bf16[128,128,128]{2,1,0:T(8,128)(2,1)S(1)} %bitcast.68, bf16[128,128,128]{2,1,0:T(8,128)(2,1)} %collective-permute-done.4.refs_1_, ...), custom_call_target="tpu_custom_call" | custom-call | flops 268435456 | bytes 655360 | tf_op jit(solution)/shard_map/direct/pallas_call | solution.py:152
  32.8 1.1 collective-permute-done.10
  34.1 2.0 %collective-permute-start.12 = (bf16[16,32,128]{2,1,0:T(8,128)(2,1)S(1)}, bf16[16,32,128]{2,1,0:T(8,128)(2,1)S(1)}, u32[]{:S(2)}, u32[]{:S(2)}) collective-permute-start(bf16[16,32,128]{2,1,0:T(8,128)(2,1)S(1)} %add_convert_fusion.2), channel_id=1, source_target_pairs={{0,8},{1,9},{2,10},{3,11},{4,12},{5,13},{6,14},{7,15},{8,0},{9,1},... | collective-permute-start | bytes 393224 | tf_op jit(solution)/shard_map/ppermute | solution.py:189
  36.1 0.2 collective-permute-start.13
  36.3 2.1 %collective-permute-done.12 = bf16[16,32,128]{2,1,0:T(8,128)(2,1)S(1)} collective-permute-done((bf16[16,32,128]{2,1,0:T(8,128)(2,1)S(1)}, bf16[16,32,128]{2,1,0:T(8,128)(2,1)S(1)}, u32[]{:S(2)}, u32[]{:S(2)}) %collective-permute-start.12) | collective-permute-done | bytes 131104 | tf_op jit(solution)/shard_map/ppermute | solution.py:189
  38.5 1.8 %collective-permute-done.13 = bf16[16,32,128]{2,1,0:T(8,128)(2,1)S(1)} collective-permute-done((bf16[16,32,128]{2,1,0:T(8,128)(2,1)S(1)}, bf16[16,32,128]{2,1,0:T(8,128)(2,1)S(1)}, u32[]{:S(2)}, u32[]{:S(2)}) %collective-permute-start.13) | collective-permute-done | bytes 131104 | tf_op jit(solution)/shard_map/ppermute | solution.py:189
  40.3 3.2 %collective-permute-start.14 = (bf16[16,32,128]{2,1,0:T(8,128)(2,1)S(1)}, bf16[16,32,128]{2,1,0:T(8,128)(2,1)S(1)}, u32[]{:S(2)}, u32[]{:S(2)}) collective-permute-start(bf16[16,32,128]{2,1,0:T(8,128)(2,1)S(1)} %get-tuple-element.63), channel_id=1, source_target_pairs={{0,16},{1,17},{2,18},{3,19},{4,20},{5,21},{6,22},{7,23},{8,24},{9,... | collective-permute-start | bytes 393224 | tf_op jit(solution)/shard_map/ppermute | solution.py:189
  43.5 3.7 %collective-permute-done.14 = bf16[16,32,128]{2,1,0:T(8,128)(2,1)S(1)} collective-permute-done((bf16[16,32,128]{2,1,0:T(8,128)(2,1)S(1)}, bf16[16,32,128]{2,1,0:T(8,128)(2,1)S(1)}, u32[]{:S(2)}, u32[]{:S(2)}) %collective-permute-start.14) | collective-permute-done | bytes 131104 | tf_op jit(solution)/shard_map/ppermute | solution.py:189
  47.3 0.6 collective-permute-start.15
  47.9 1.0 collective-permute-start.21
  48.9 2.5 %collective-permute-start.20 = (bf16[16,32,128]{2,1,0:T(8,128)(2,1)S(1)}, bf16[16,32,128]{2,1,0:T(8,128)(2,1)S(1)}, u32[]{:S(2)}, u32[]{:S(2)}) collective-permute-start(bf16[16,32,128]{2,1,0:T(8,128)(2,1)S(1)} %get-tuple-element.61), channel_id=1, source_target_pairs={{0,4},{1,5},{2,6},{3,7},{4,0},{5,1},{6,2},{7,3},{8,12},{9,13},{10,... | collective-permute-start | bytes 393224 | tf_op jit(solution)/shard_map/ppermute | solution.py:189
  51.5 1.2 %collective-permute-start.19 = (bf16[16,32,128]{2,1,0:T(8,128)(2,1)S(1)}, bf16[16,32,128]{2,1,0:T(8,128)(2,1)S(1)}, u32[]{:S(2)}, u32[]{:S(2)}) collective-permute-start(bf16[16,32,128]{2,1,0:T(8,128)(2,1)S(1)} %get-tuple-element.61), channel_id=1, source_target_pairs={{0,8},{1,9},{2,10},{3,11},{4,12},{5,13},{6,14},{7,15},{8,0},{9,1},... | collective-permute-start | bytes 393224 | tf_op jit(solution)/shard_map/ppermute | solution.py:189
  52.7 2.7 %transposed.4 = (f32[16,32,128]{2,1,0:T(8,128)S(1)}, f32[16,32,128]{2,1,0:T(8,128)S(1)}, bf16[16,32,128]{2,1,0:T(8,128)(2,1)S(1)}, bf16[16,32,128]{2,1,0:T(8,128)(2,1)S(1)}) custom-call(s32[1152]{0:T(1024)S(1)} %concatenate.50.meta_in, bf16[16,32,128]{2,1,0:T(8,128)(2,1)S(1)} %broadcast_select_fusion.1.vecs_in, bf16[128,128,128]{2,1,0:T(8,128)(2,1)S(1)} %bitcast.69, ...), custom_call_target="tpu_custom_call" | custom-call | flops 268435456 | bytes 655360 | tf_op jit(solution)/shard_map/transposed/pallas_call | solution.py:152
  55.3 2.4 %collective-permute-start.16 = (bf16[16,32,128]{2,1,0:T(8,128)(2,1)S(1)}, bf16[16,32,128]{2,1,0:T(8,128)(2,1)S(1)}, u32[]{:S(2)}, u32[]{:S(2)}) collective-permute-start(bf16[16,32,128]{2,1,0:T(8,128)(2,1)S(1)} %get-tuple-element.50.refs_2_), channel_id=1, source_target_pairs={{0,4},{1,5},{2,6},{3,7},{4,0},{5,1},{6,2},{7,3},{8,12},{9,13},{10,... | collective-permute-start | bytes 393224 | tf_op jit(solution)/shard_map/ppermute | solution.py:189
  57.9 2.7 %direct.4 = bf16[16,32,128]{2,1,0:T(8,128)(2,1)S(1)} custom-call(s32[1152]{0:T(1024)S(1)} %concatenate.50.meta_in, bf16[64,32,128]{2,1,0:T(8,128)(2,1)S(1)} %pad_maximum_fusion.1.vecs_in, bf16[128,128,128]{2,1,0:T(8,128)(2,1)S(1)} %bitcast.70, bf16[128,128,128]{2,1,0:T(8,128)(2,1)} %collective-permute-done.4.refs_1_, ...), custom_call_target="tpu_custom_call" | custom-call | flops 268435456 | bytes 655360 | tf_op jit(solution)/shard_map/direct/pallas_call | solution.py:152
  60.6 2.7 %collective-permute-start.22 = (bf16[16,32,128]{2,1,0:T(8,128)(2,1)S(1)}, bf16[16,32,128]{2,1,0:T(8,128)(2,1)S(1)}, u32[]{:S(2)}, u32[]{:S(2)}) collective-permute-start(bf16[16,32,128]{2,1,0:T(8,128)(2,1)S(1)} %direct.4), channel_id=1, source_target_pairs={{0,2},{1,3},{2,0},{3,1},{4,6},{5,7},{6,4},{7,5},{8,10},{9,11},{10,... | collective-permute-start | bytes 393224 | tf_op jit(solution)/shard_map/ppermute | solution.py:189
  63.5 2.2 %collective-permute-done.22 = bf16[16,32,128]{2,1,0:T(8,128)(2,1)S(1)} collective-permute-done((bf16[16,32,128]{2,1,0:T(8,128)(2,1)S(1)}, bf16[16,32,128]{2,1,0:T(8,128)(2,1)S(1)}, u32[]{:S(2)}, u32[]{:S(2)}) %collective-permute-start.22) | collective-permute-done | bytes 131104 | tf_op jit(solution)/shard_map/ppermute | solution.py:189
  65.7 1.6 %collective-permute-done.18 = bf16[16,32,128]{2,1,0:T(8,128)(2,1)S(1)} collective-permute-done((bf16[16,32,128]{2,1,0:T(8,128)(2,1)S(1)}, bf16[16,32,128]{2,1,0:T(8,128)(2,1)S(1)}, u32[]{:S(2)}, u32[]{:S(2)}) %collective-permute-start.18) | collective-permute-done | bytes 131104 | tf_op jit(solution)/shard_map/ppermute | solution.py:189
  67.4 1.0 collective-permute-start.23
  68.4 5.0 %collective-permute-done.23 = bf16[16,32,128]{2,1,0:T(8,128)(2,1)S(1)} collective-permute-done((bf16[16,32,128]{2,1,0:T(8,128)(2,1)S(1)}, bf16[16,32,128]{2,1,0:T(8,128)(2,1)S(1)}, u32[]{:S(2)}, u32[]{:S(2)}) %collective-permute-start.23) | collective-permute-done | bytes 131104 | tf_op jit(solution)/shard_map/ppermute | solution.py:189
  73.4 0.1 multiply_convert_fusion
  73.6 1.1 collective-permute-start.30
  74.8 0.7 collective-permute-start.29
  75.5 0.9 collective-permute-start.28
  76.4 1.4 %collective-permute-done.24 = bf16[16,32,128]{2,1,0:T(8,128)(2,1)S(1)} collective-permute-done((bf16[16,32,128]{2,1,0:T(8,128)(2,1)S(1)}, bf16[16,32,128]{2,1,0:T(8,128)(2,1)S(1)}, u32[]{:S(2)}, u32[]{:S(2)}) %collective-permute-start.24) | collective-permute-done | bytes 131104 | tf_op jit(solution)/shard_map/ppermute | solution.py:189
  77.8 2.7 %transposed.5 = (f32[16,32,128]{2,1,0:T(8,128)S(1)}, f32[16,32,128]{2,1,0:T(8,128)S(1)}, bf16[16,32,128]{2,1,0:T(8,128)(2,1)S(1)}, bf16[16,32,128]{2,1,0:T(8,128)(2,1)S(1)}) custom-call(s32[1152]{0:T(1024)S(1)} %concatenate.50.meta_in, bf16[16,32,128]{2,1,0:T(8,128)(2,1)S(1)} %broadcast_select_fusion.vecs_in, bf16[128,128,128]{2,1,0:T(8,128)(2,1)S(1)} %bitcast.71, ...), custom_call_target="tpu_custom_call" | custom-call | flops 268435456 | bytes 655360 | tf_op jit(solution)/shard_map/transposed/pallas_call | solution.py:152
  80.4 0.3 collective-permute-start.25
  80.7 1.3 %collective-permute-start.26 = (bf16[16,32,128]{2,1,0:T(8,128)(2,1)S(1)}, bf16[16,32,128]{2,1,0:T(8,128)(2,1)S(1)}, u32[]{:S(2)}, u32[]{:S(2)}) collective-permute-start(bf16[16,32,128]{2,1,0:T(8,128)(2,1)S(1)} %get-tuple-element.56.refs_3_), channel_id=1, source_target_pairs={{0,4},{1,5},{2,6},{3,7},{4,0},{5,1},{6,2},{7,3},{8,12},{9,13},{10,... | collective-permute-start | bytes 393224 | tf_op jit(solution)/shard_map/ppermute | solution.py:189
  82.1 2.7 %direct.5 = bf16[16,32,128]{2,1,0:T(8,128)(2,1)S(1)} custom-call(s32[1152]{0:T(1024)S(1)} %concatenate.50.meta_in, bf16[64,32,128]{2,1,0:T(8,128)(2,1)S(1)} %pad_maximum_fusion.2.vecs_in, bf16[128,128,128]{2,1,0:T(8,128)(2,1)S(1)} %bitcast.72, bf16[128,128,128]{2,1,0:T(8,128)(2,1)} %collective-permute-done.4.refs_1_, ...), custom_call_target="tpu_custom_call" | custom-call | flops 268435456 | bytes 655360 | tf_op jit(solution)/shard_map/direct/pallas_call | solution.py:152
  84.8 2.2 %collective-permute-start.31 = (bf16[16,32,128]{2,1,0:T(8,128)(2,1)S(1)}, bf16[16,32,128]{2,1,0:T(8,128)(2,1)S(1)}, u32[]{:S(2)}, u32[]{:S(2)}) collective-permute-start(bf16[16,32,128]{2,1,0:T(8,128)(2,1)S(1)} %direct.5), channel_id=1, source_target_pairs={{0,2},{1,3},{2,0},{3,1},{4,6},{5,7},{6,4},{7,5},{8,10},{9,11},{10,... | collective-permute-start | bytes 393224 | tf_op jit(solution)/shard_map/ppermute | solution.py:189
  87.0 1.5 %collective-permute-done.26 = bf16[16,32,128]{2,1,0:T(8,128)(2,1)S(1)} collective-permute-done((bf16[16,32,128]{2,1,0:T(8,128)(2,1)S(1)}, bf16[16,32,128]{2,1,0:T(8,128)(2,1)S(1)}, u32[]{:S(2)}, u32[]{:S(2)}) %collective-permute-start.26) | collective-permute-done | bytes 131104 | tf_op jit(solution)/shard_map/ppermute | solution.py:189
  88.6 0.7 collective-permute-done.31
  89.4 3.4 %collective-permute-done.27 = bf16[16,32,128]{2,1,0:T(8,128)(2,1)S(1)} collective-permute-done((bf16[16,32,128]{2,1,0:T(8,128)(2,1)S(1)}, bf16[16,32,128]{2,1,0:T(8,128)(2,1)S(1)}, u32[]{:S(2)}, u32[]{:S(2)}) %collective-permute-start.27) | collective-permute-done | bytes 131104 | tf_op jit(solution)/shard_map/ppermute | solution.py:189
  92.9 0.3 collective-permute-start.32
  93.1 4.2 %collective-permute-done.32 = bf16[8,32,128]{2,1,0:T(8,128)(2,1)S(1)} collective-permute-done((bf16[8,32,128]{2,1,0:T(8,128)(2,1)S(1)}, bf16[8,32,128]{2,1,0:T(8,128)(2,1)S(1)}, u32[]{:S(2)}, u32[]{:S(2)}) %collective-permute-start.32) | collective-permute-done | bytes 65568 | tf_op jit(solution)/shard_map/ppermute | solution.py:189
  97.4 7.7 %collective-permute-start.34 = (f32[4,32,128]{2,1,0:T(8,128)S(1)}, f32[4,32,128]{2,1,0:T(8,128)S(1)}, u32[]{:S(2)}, u32[]{:S(2)}) collective-permute-start(f32[4,32,128]{2,1,0:T(8,128)S(1)} %get-tuple-element.81), channel_id=1, source_target_pairs={{1,0},{0,1},{17,2},{16,3},{5,4},{4,5},{21,6},{20,7},{9,8},{8,9},{2... | collective-permute-start | bytes 196616 | tf_op jit(solution)/shard_map/ppermute | solution.py:189
  105.1 3.6 %collective-permute-start.33 = (f32[4,32,128]{2,1,0:T(8,128)S(1)}, f32[4,32,128]{2,1,0:T(8,128)S(1)}, u32[]{:S(2)}, u32[]{:S(2)}) collective-permute-start(f32[4,32,128]{2,1,0:T(8,128)S(1)} %get-tuple-element.82), channel_id=1, source_target_pairs={{0,0},{1,1},{16,2},{17,3},{4,4},{5,5},{20,6},{21,7},{8,8},{9,9},{2... | collective-permute-start | bytes 196616 | tf_op jit(solution)/shard_map/ppermute | solution.py:189
  108.7 0.3 collective-permute-done.34
  109.0 5.5 %collective-permute-done.33 = f32[4,32,128]{2,1,0:T(8,128)S(1)} collective-permute-done((f32[4,32,128]{2,1,0:T(8,128)S(1)}, f32[4,32,128]{2,1,0:T(8,128)S(1)}, u32[]{:S(2)}, u32[]{:S(2)}) %collective-permute-start.33) | collective-permute-done | bytes 65568 | tf_op jit(solution)/shard_map/ppermute | solution.py:189
  114.6 0.7 copy.15
  (72 shorter events, 1.8 us)
Async XLA Ops:
  0.0 9.6 %collective-permute-start.4 = (bf16[128,128,128]{2,1,0:T(8,128)(2,1)}, bf16[128,128,128]{2,1,0:T(8,128)(2,1)}, u32[]{:S(2)}, u32[]{:S(2)}) collective-permute-start(bf16[128,128,128]{2,1,0:T(8,128)(2,1)} %bitcast.66), channel_id=1, source_target_pairs={{0,1},{1,0},{2,3},{3,2},{4,5},{5,4},{6,7},{7,6},{8,9},{9,8},{10,11... | collective-permute-start | bytes 12582920 | tf_op jit(solution)/shard_map/ppermute | solution.py:189
  2.4 7.2 %collective-permute-start.2 = (f32[4,40,128]{2,1,0:T(8,128)S(1)}, f32[4,40,128]{2,1,0:T(8,128)S(1)}, u32[]{:S(2)}, u32[]{:S(2)}) collective-permute-start(f32[4,40,128]{2,1,0:T(8,128)S(1)} %get-tuple-element.77), channel_id=1, source_target_pairs={{0,1},{1,0},{2,3},{3,2},{4,5},{5,4},{6,7},{7,6},{8,9},{9,8},{10,11... | collective-permute-start | bytes 245768 | tf_op jit(solution)/shard_map/ppermute | solution.py:189
  2.4 7.1 %collective-permute-start.1 = (f32[4,40,128]{2,1,0:T(8,128)S(1)}, f32[4,40,128]{2,1,0:T(8,128)S(1)}, u32[]{:S(2)}, u32[]{:S(2)}) collective-permute-start(f32[4,40,128]{2,1,0:T(8,128)S(1)} %get-tuple-element.77), channel_id=1, source_target_pairs={{0,3},{1,2},{2,1},{3,0},{4,7},{5,6},{6,5},{7,4},{8,11},{9,10},{10,... | collective-permute-start | bytes 245768 | tf_op jit(solution)/shard_map/ppermute | solution.py:189
  3.8 3.7 %collective-permute-start.3 = (s32[257]{0:T(512)S(1)}, s32[257]{0:T(512)S(1)}, u32[]{:S(2)}, u32[]{:S(2)}) collective-permute-start(s32[257]{0:T(512)S(1)} %pad_add_fusion), channel_id=1, source_target_pairs={{0,1},{1,0},{2,3},{3,2},{4,5},{5,4},{6,7},{7,6},{8,9},{9,8},{10,11... | collective-permute-start | bytes 3092 | tf_op jit(solution)/shard_map/ppermute | solution.py:189
  4.3 5.3 %collective-permute-start = (f32[4,40,128]{2,1,0:T(8,128)S(1)}, f32[4,40,128]{2,1,0:T(8,128)S(1)}, u32[]{:S(2)}, u32[]{:S(2)}) collective-permute-start(f32[4,40,128]{2,1,0:T(8,128)S(1)} %get-tuple-element.78), channel_id=1, source_target_pairs={{0,2},{1,3},{2,0},{3,1},{4,6},{5,7},{6,4},{7,5},{8,10},{9,11},{10,... | collective-permute-start | bytes 245768 | tf_op jit(solution)/shard_map/ppermute | solution.py:189
  9.7 8.5 %collective-permute-start.6 = (bf16[16,32,128]{2,1,0:T(8,128)(2,1)S(1)}, bf16[16,32,128]{2,1,0:T(8,128)(2,1)S(1)}, u32[]{:S(2)}, u32[]{:S(2)}) collective-permute-start(bf16[16,32,128]{2,1,0:T(8,128)(2,1)S(1)} %multiply_convert_fusion.2.vecs_in), channel_id=1, source_target_pairs={{0,16},{1,17},{2,18},{3,19},{4,20},{5,21},{6,22},{7,23},{8,24},{9,... | collective-permute-start | bytes 393224 | tf_op jit(solution)/shard_map/ppermute | solution.py:189
  12.1 2.2 %copy-start = (bf16[1,1,128,128,128]{4,3,2,1,0:T(8,128)(2,1)S(1)}, bf16[1,1,128,128,128]{4,3,2,1,0:T(8,128)(2,1)}, u32[]{:S(2)}) copy-start(bf16[1,1,128,128,128]{4,3,2,1,0:T(8,128)(2,1)} %param.7) | copy-start | bytes 12582916
  18.2 3.9 %collective-permute-start.7 = (bf16[16,32,128]{2,1,0:T(8,128)(2,1)S(1)}, bf16[16,32,128]{2,1,0:T(8,128)(2,1)S(1)}, u32[]{:S(2)}, u32[]{:S(2)}) collective-permute-start(bf16[16,32,128]{2,1,0:T(8,128)(2,1)S(1)} %maximum_select_fusion.1), channel_id=1, source_target_pairs={{0,8},{1,9},{2,10},{3,11},{4,12},{5,13},{6,14},{7,15},{8,0},{9,1},... | collective-permute-start | bytes 393224 | tf_op jit(solution)/shard_map/ppermute | solution.py:189
  19.5 8.0 %collective-permute-start.9 = (bf16[16,32,128]{2,1,0:T(8,128)(2,1)S(1)}, bf16[16,32,128]{2,1,0:T(8,128)(2,1)S(1)}, u32[]{:S(2)}, u32[]{:S(2)}) collective-permute-start(bf16[16,32,128]{2,1,0:T(8,128)(2,1)S(1)} %maximum_select_fusion.1), channel_id=1, source_target_pairs={{0,12},{1,13},{2,14},{3,15},{4,8},{5,9},{6,10},{7,11},{8,4},{9,5},... | collective-permute-start | bytes 393224 | tf_op jit(solution)/shard_map/ppermute | solution.py:189
  20.8 7.0 %collective-permute-start.8 = (bf16[16,32,128]{2,1,0:T(8,128)(2,1)S(1)}, bf16[16,32,128]{2,1,0:T(8,128)(2,1)S(1)}, u32[]{:S(2)}, u32[]{:S(2)}) collective-permute-start(bf16[16,32,128]{2,1,0:T(8,128)(2,1)S(1)} %maximum_select_fusion.1), channel_id=1, source_target_pairs={{0,4},{1,5},{2,6},{3,7},{4,0},{5,1},{6,2},{7,3},{8,12},{9,13},{10,... | collective-permute-start | bytes 393224 | tf_op jit(solution)/shard_map/ppermute | solution.py:189
  22.1 11.8 %collective-permute-start.10 = (bf16[16,48,128]{2,1,0:T(8,128)(2,1)S(1)}, bf16[16,48,128]{2,1,0:T(8,128)(2,1)S(1)}, u32[]{:S(2)}, u32[]{:S(2)}) collective-permute-start(bf16[16,48,128]{2,1,0:T(8,128)(2,1)S(1)} %pad_maximum_fusion.4), channel_id=1, source_target_pairs={{0,16},{1,17},{2,18},{3,19},{4,20},{5,21},{6,22},{7,23},{8,24},{9,... | collective-permute-start | bytes 589832 | tf_op jit(solution)/shard_map/ppermute | solution.py:189
  26.0 6.9 %collective-permute-start.5 = (bf16[16,32,128]{2,1,0:T(8,128)(2,1)S(1)}, bf16[16,32,128]{2,1,0:T(8,128)(2,1)S(1)}, u32[]{:S(2)}, u32[]{:S(2)}) collective-permute-start(bf16[16,32,128]{2,1,0:T(8,128)(2,1)S(1)} %get-tuple-element.42.refs_3_), channel_id=1, source_target_pairs={{0,4},{1,5},{2,6},{3,7},{4,0},{5,1},{6,2},{7,3},{8,12},{9,13},{10,... | collective-permute-start | bytes 393224 | tf_op jit(solution)/shard_map/ppermute | solution.py:189
  27.2 9.1 %collective-permute-start.11 = (bf16[16,32,128]{2,1,0:T(8,128)(2,1)S(1)}, bf16[16,32,128]{2,1,0:T(8,128)(2,1)S(1)}, u32[]{:S(2)}, u32[]{:S(2)}) collective-permute-start(bf16[16,32,128]{2,1,0:T(8,128)(2,1)S(1)} %get-tuple-element.41.refs_2_), channel_id=1, source_target_pairs={{0,4},{1,5},{2,6},{3,7},{4,0},{5,1},{6,2},{7,3},{8,12},{9,13},{10,... | collective-permute-start | bytes 393224 | tf_op jit(solution)/shard_map/ppermute | solution.py:189
  27.9 2.2 %copy-start.1 = (bf16[1,1,128,128,128]{4,3,2,1,0:T(8,128)(2,1)S(1)}, bf16[1,1,128,128,128]{4,3,2,1,0:T(8,128)(2,1)}, u32[]{:S(2)}) copy-start(bf16[1,1,128,128,128]{4,3,2,1,0:T(8,128)(2,1)} %param.7) | copy-start | bytes 12582916
  34.1 4.4 %collective-permute-start.12 = (bf16[16,32,128]{2,1,0:T(8,128)(2,1)S(1)}, bf16[16,32,128]{2,1,0:T(8,128)(2,1)S(1)}, u32[]{:S(2)}, u32[]{:S(2)}) collective-permute-start(bf16[16,32,128]{2,1,0:T(8,128)(2,1)S(1)} %add_convert_fusion.2), channel_id=1, source_target_pairs={{0,8},{1,9},{2,10},{3,11},{4,12},{5,13},{6,14},{7,15},{8,0},{9,1},... | collective-permute-start | bytes 393224 | tf_op jit(solution)/shard_map/ppermute | solution.py:189
  36.1 4.1 %collective-permute-start.13 = (bf16[16,32,128]{2,1,0:T(8,128)(2,1)S(1)}, bf16[16,32,128]{2,1,0:T(8,128)(2,1)S(1)}, u32[]{:S(2)}, u32[]{:S(2)}) collective-permute-start(bf16[16,32,128]{2,1,0:T(8,128)(2,1)S(1)} %direct.3), channel_id=1, source_target_pairs={{0,2},{1,3},{2,0},{3,1},{4,6},{5,7},{6,4},{7,5},{8,10},{9,11},{10,... | collective-permute-start | bytes 393224 | tf_op jit(solution)/shard_map/ppermute | solution.py:189
  40.3 6.9 %collective-permute-start.14 = (bf16[16,32,128]{2,1,0:T(8,128)(2,1)S(1)}, bf16[16,32,128]{2,1,0:T(8,128)(2,1)S(1)}, u32[]{:S(2)}, u32[]{:S(2)}) collective-permute-start(bf16[16,32,128]{2,1,0:T(8,128)(2,1)S(1)} %get-tuple-element.63), channel_id=1, source_target_pairs={{0,16},{1,17},{2,18},{3,19},{4,20},{5,21},{6,22},{7,23},{8,24},{9,... | collective-permute-start | bytes 393224 | tf_op jit(solution)/shard_map/ppermute | solution.py:189
  47.3 5.4 %collective-permute-start.15 = (bf16[16,32,128]{2,1,0:T(8,128)(2,1)S(1)}, bf16[16,32,128]{2,1,0:T(8,128)(2,1)S(1)}, u32[]{:S(2)}, u32[]{:S(2)}) collective-permute-start(bf16[16,32,128]{2,1,0:T(8,128)(2,1)S(1)} %get-tuple-element.61), channel_id=1, source_target_pairs={{0,2},{1,3},{2,0},{3,1},{4,6},{5,7},{6,4},{7,5},{8,10},{9,11},{10,... | collective-permute-start | bytes 393224 | tf_op jit(solution)/shard_map/ppermute | solution.py:189
  47.9 9.9 %collective-permute-start.21 = (bf16[16,32,128]{2,1,0:T(8,128)(2,1)S(1)}, bf16[16,32,128]{2,1,0:T(8,128)(2,1)S(1)}, u32[]{:S(2)}, u32[]{:S(2)}) collective-permute-start(bf16[16,32,128]{2,1,0:T(8,128)(2,1)S(1)} %get-tuple-element.61), channel_id=1, source_target_pairs={{0,12},{1,13},{2,14},{3,15},{4,8},{5,9},{6,10},{7,11},{8,4},{9,5},... | collective-permute-start | bytes 393224 | tf_op jit(solution)/shard_map/ppermute | solution.py:189
  48.9 8.9 %collective-permute-start.20 = (bf16[16,32,128]{2,1,0:T(8,128)(2,1)S(1)}, bf16[16,32,128]{2,1,0:T(8,128)(2,1)S(1)}, u32[]{:S(2)}, u32[]{:S(2)}) collective-permute-start(bf16[16,32,128]{2,1,0:T(8,128)(2,1)S(1)} %get-tuple-element.61), channel_id=1, source_target_pairs={{0,4},{1,5},{2,6},{3,7},{4,0},{5,1},{6,2},{7,3},{8,12},{9,13},{10,... | collective-permute-start | bytes 393224 | tf_op jit(solution)/shard_map/ppermute | solution.py:189
  51.5 6.4 %collective-permute-start.19 = (bf16[16,32,128]{2,1,0:T(8,128)(2,1)S(1)}, bf16[16,32,128]{2,1,0:T(8,128)(2,1)S(1)}, u32[]{:S(2)}, u32[]{:S(2)}) collective-permute-start(bf16[16,32,128]{2,1,0:T(8,128)(2,1)S(1)} %get-tuple-element.61), channel_id=1, source_target_pairs={{0,8},{1,9},{2,10},{3,11},{4,12},{5,13},{6,14},{7,15},{8,0},{9,1},... | collective-permute-start | bytes 393224 | tf_op jit(solution)/shard_map/ppermute | solution.py:189
  55.3 10.4 %collective-permute-start.16 = (bf16[16,32,128]{2,1,0:T(8,128)(2,1)S(1)}, bf16[16,32,128]{2,1,0:T(8,128)(2,1)S(1)}, u32[]{:S(2)}, u32[]{:S(2)}) collective-permute-start(bf16[16,32,128]{2,1,0:T(8,128)(2,1)S(1)} %get-tuple-element.50.refs_2_), channel_id=1, source_target_pairs={{0,4},{1,5},{2,6},{3,7},{4,0},{5,1},{6,2},{7,3},{8,12},{9,13},{10,... | collective-permute-start | bytes 393224 | tf_op jit(solution)/shard_map/ppermute | solution.py:189
  57.8 5.6 %collective-permute-start.17 = (bf16[16,32,128]{2,1,0:T(8,128)(2,1)S(1)}, bf16[16,32,128]{2,1,0:T(8,128)(2,1)S(1)}, u32[]{:S(2)}, u32[]{:S(2)}) collective-permute-start(bf16[16,32,128]{2,1,0:T(8,128)(2,1)S(1)} %get-tuple-element.52.refs_3_), channel_id=1, source_target_pairs={{0,4},{1,5},{2,6},{3,7},{4,0},{5,1},{6,2},{7,3},{8,12},{9,13},{10,... | collective-permute-start | bytes 393224 | tf_op jit(solution)/shard_map/ppermute | solution.py:189
  60.6 5.1 %collective-permute-start.22 = (bf16[16,32,128]{2,1,0:T(8,128)(2,1)S(1)}, bf16[16,32,128]{2,1,0:T(8,128)(2,1)S(1)}, u32[]{:S(2)}, u32[]{:S(2)}) collective-permute-start(bf16[16,32,128]{2,1,0:T(8,128)(2,1)S(1)} %direct.4), channel_id=1, source_target_pairs={{0,2},{1,3},{2,0},{3,1},{4,6},{5,7},{6,4},{7,5},{8,10},{9,11},{10,... | collective-permute-start | bytes 393224 | tf_op jit(solution)/shard_map/ppermute | solution.py:189
  63.4 3.9 %collective-permute-start.18 = (bf16[16,32,128]{2,1,0:T(8,128)(2,1)S(1)}, bf16[16,32,128]{2,1,0:T(8,128)(2,1)S(1)}, u32[]{:S(2)}, u32[]{:S(2)}) collective-permute-start(bf16[16,32,128]{2,1,0:T(8,128)(2,1)S(1)} %add_convert_fusion.1), channel_id=1, source_target_pairs={{0,8},{1,9},{2,10},{3,11},{4,12},{5,13},{6,14},{7,15},{8,0},{9,1},... | collective-permute-start | bytes 393224 | tf_op jit(solution)/shard_map/ppermute | solution.py:189
  67.4 6.0 %collective-permute-start.23 = (bf16[16,32,128]{2,1,0:T(8,128)(2,1)S(1)}, bf16[16,32,128]{2,1,0:T(8,128)(2,1)S(1)}, u32[]{:S(2)}, u32[]{:S(2)}) collective-permute-start(bf16[16,32,128]{2,1,0:T(8,128)(2,1)S(1)} %get-tuple-element.59), channel_id=1, source_target_pairs={{0,16},{1,17},{2,18},{3,19},{4,20},{5,21},{6,22},{7,23},{8,24},{9,... | collective-permute-start | bytes 393224 | tf_op jit(solution)/shard_map/ppermute | solution.py:189
  73.6 4.2 %collective-permute-start.24 = (bf16[16,32,128]{2,1,0:T(8,128)(2,1)S(1)}, bf16[16,32,128]{2,1,0:T(8,128)(2,1)S(1)}, u32[]{:S(2)}, u32[]{:S(2)}) collective-permute-start(bf16[16,32,128]{2,1,0:T(8,128)(2,1)S(1)} %get-tuple-element.57), channel_id=1, source_target_pairs={{0,2},{1,3},{2,0},{3,1},{4,6},{5,7},{6,4},{7,5},{8,10},{9,11},{10,... | collective-permute-start | bytes 393224 | tf_op jit(solution)/shard_map/ppermute | solution.py:189
  73.6 8.3 %collective-permute-start.30 = (bf16[16,32,128]{2,1,0:T(8,128)(2,1)S(1)}, bf16[16,32,128]{2,1,0:T(8,128)(2,1)S(1)}, u32[]{:S(2)}, u32[]{:S(2)}) collective-permute-start(bf16[16,32,128]{2,1,0:T(8,128)(2,1)S(1)} %get-tuple-element.57), channel_id=1, source_target_pairs={{0,12},{1,13},{2,14},{3,15},{4,8},{5,9},{6,10},{7,11},{8,4},{9,5},... | collective-permute-start | bytes 393224 | tf_op jit(solution)/shard_map/ppermute | solution.py:189
  74.8 7.2 %collective-permute-start.29 = (bf16[16,32,128]{2,1,0:T(8,128)(2,1)S(1)}, bf16[16,32,128]{2,1,0:T(8,128)(2,1)S(1)}, u32[]{:S(2)}, u32[]{:S(2)}) collective-permute-start(bf16[16,32,128]{2,1,0:T(8,128)(2,1)S(1)} %get-tuple-element.57), channel_id=1, source_target_pairs={{0,4},{1,5},{2,6},{3,7},{4,0},{5,1},{6,2},{7,3},{8,12},{9,13},{10,... | collective-permute-start | bytes 393224 | tf_op jit(solution)/shard_map/ppermute | solution.py:189
  75.5 6.5 %collective-permute-start.28 = (bf16[16,32,128]{2,1,0:T(8,128)(2,1)S(1)}, bf16[16,32,128]{2,1,0:T(8,128)(2,1)S(1)}, u32[]{:S(2)}, u32[]{:S(2)}) collective-permute-start(bf16[16,32,128]{2,1,0:T(8,128)(2,1)S(1)} %get-tuple-element.57), channel_id=1, source_target_pairs={{0,8},{1,9},{2,10},{3,11},{4,12},{5,13},{6,14},{7,15},{8,0},{9,1},... | collective-permute-start | bytes 393224 | tf_op jit(solution)/shard_map/ppermute | solution.py:189
  80.4 8.9 %collective-permute-start.25 = (bf16[16,32,128]{2,1,0:T(8,128)(2,1)S(1)}, bf16[16,32,128]{2,1,0:T(8,128)(2,1)S(1)}, u32[]{:S(2)}, u32[]{:S(2)}) collective-permute-start(bf16[16,32,128]{2,1,0:T(8,128)(2,1)S(1)} %get-tuple-element.54.refs_2_), channel_id=1, source_target_pairs={{0,4},{1,5},{2,6},{3,7},{4,0},{5,1},{6,2},{7,3},{8,12},{9,13},{10,... | collective-permute-start | bytes 393224 | tf_op jit(solution)/shard_map/ppermute | solution.py:189
  80.7 7.8 %collective-permute-start.26 = (bf16[16,32,128]{2,1,0:T(8,128)(2,1)S(1)}, bf16[16,32,128]{2,1,0:T(8,128)(2,1)S(1)}, u32[]{:S(2)}, u32[]{:S(2)}) collective-permute-start(bf16[16,32,128]{2,1,0:T(8,128)(2,1)S(1)} %get-tuple-element.56.refs_3_), channel_id=1, source_target_pairs={{0,4},{1,5},{2,6},{3,7},{4,0},{5,1},{6,2},{7,3},{8,12},{9,13},{10,... | collective-permute-start | bytes 393224 | tf_op jit(solution)/shard_map/ppermute | solution.py:189
  84.8 4.6 %collective-permute-start.31 = (bf16[16,32,128]{2,1,0:T(8,128)(2,1)S(1)}, bf16[16,32,128]{2,1,0:T(8,128)(2,1)S(1)}, u32[]{:S(2)}, u32[]{:S(2)}) collective-permute-start(bf16[16,32,128]{2,1,0:T(8,128)(2,1)S(1)} %direct.5), channel_id=1, source_target_pairs={{0,2},{1,3},{2,0},{3,1},{4,6},{5,7},{6,4},{7,5},{8,10},{9,11},{10,... | collective-permute-start | bytes 393224 | tf_op jit(solution)/shard_map/ppermute | solution.py:189
  88.6 4.2 %collective-permute-start.27 = (bf16[16,32,128]{2,1,0:T(8,128)(2,1)S(1)}, bf16[16,32,128]{2,1,0:T(8,128)(2,1)S(1)}, u32[]{:S(2)}, u32[]{:S(2)}) collective-permute-start(bf16[16,32,128]{2,1,0:T(8,128)(2,1)S(1)} %add_convert_fusion), channel_id=1, source_target_pairs={{0,8},{1,9},{2,10},{3,11},{4,12},{5,13},{6,14},{7,15},{8,0},{9,1},... | collective-permute-start | bytes 393224 | tf_op jit(solution)/shard_map/ppermute | solution.py:189
  92.9 4.5 %collective-permute-start.32 = (bf16[8,32,128]{2,1,0:T(8,128)(2,1)S(1)}, bf16[8,32,128]{2,1,0:T(8,128)(2,1)S(1)}, u32[]{:S(2)}, u32[]{:S(2)}) collective-permute-start(bf16[8,32,128]{2,1,0:T(8,128)(2,1)S(1)} %slice.200), channel_id=1, source_target_pairs={{0,16},{1,17},{2,18},{3,19},{4,20},{5,21},{6,22},{7,23},{8,24},{9,... | collective-permute-start | bytes 196616 | tf_op jit(solution)/shard_map/ppermute | solution.py:189
  97.4 11.6 %collective-permute-start.34 = (f32[4,32,128]{2,1,0:T(8,128)S(1)}, f32[4,32,128]{2,1,0:T(8,128)S(1)}, u32[]{:S(2)}, u32[]{:S(2)}) collective-permute-start(f32[4,32,128]{2,1,0:T(8,128)S(1)} %get-tuple-element.81), channel_id=1, source_target_pairs={{1,0},{0,1},{17,2},{16,3},{5,4},{4,5},{21,6},{20,7},{9,8},{8,9},{2... | collective-permute-start | bytes 196616 | tf_op jit(solution)/shard_map/ppermute | solution.py:189
  105.1 9.3 %collective-permute-start.33 = (f32[4,32,128]{2,1,0:T(8,128)S(1)}, f32[4,32,128]{2,1,0:T(8,128)S(1)}, u32[]{:S(2)}, u32[]{:S(2)}) collective-permute-start(f32[4,32,128]{2,1,0:T(8,128)S(1)} %get-tuple-element.82), channel_id=1, source_target_pairs={{0,0},{1,1},{16,2},{17,3},{4,4},{5,5},{20,6},{21,7},{8,8},{9,9},{2... | collective-permute-start | bytes 196616 | tf_op jit(solution)/shard_map/ppermute | solution.py:189
where the time goes:
time: 115 us
  starting transfers between devices  48.3 us (42%)
  waiting for transfers between devices  38.2 us (33%)
  Pallas kernels  16.1 us (14%)
  local copies, waits for them, and re-layouts  8.14 us (7%)
  other arithmetic  3.33 us (3%)
    ppermute x35, starting transfers between devices, send(): return lax.ppermute(x, AXES, pairs)  48.3 us
    ppermute x35, waiting for transfers between devices, send(): return lax.ppermute(x, AXES, pairs)  38.2 us
    pallas_call x6, Pallas kernels, products(): pl.pallas_call(functools.partial(product_kernel, transpose, cap, n_out, l...  16.1 us
    unnamed x8, local copies, waits for them, and re-layouts  5.04 us
  transfers between devices with their start and end apart: 35, of which 18 were waited for; matrix products, arithmetic and copies ran while one was open for 5% of the time, Pallas kernels for 14%

commit v1 on v0

--- a/solution.py
+++ b/solution.py
@@ -14,7 +14,7 @@
 
 UNROLL = 64
 PACK = 4
-VMEM_LIMIT = 16 * 1024 * 1024
+VMEM_LIMIT = 24 * 1024 * 1024
 AXES = ("row", "col")
 PAD = 8
 

time: 115 us -> 115 us (level)
  transfers between devices with their start and end apart: 35 -> 35, of which waited for: 18 -> 16; matrix products, arithmetic and copies ran while one was open for 5% -> 5% of each run, Pallas kernels for 14% -> 14%
where the time goes in v1:
time: 115 us; the launch traced here: 114 us
  starting transfers between devices  48.1 us (42%)
  waiting for transfers between devices  37.4 us (33%)
  Pallas kernels  16.2 us (14%)
  local copies, waits for them, and re-layouts  8.14 us (7%)
  other arithmetic  3.33 us (3%)
    ppermute x35, starting transfers between devices, send(): return lax.ppermute(x, AXES, pairs)  48.1 us
    ppermute x35, waiting for transfers between devices, send(): return lax.ppermute(x, AXES, pairs)  37.4 us
    pallas_call x6, Pallas kernels, products(): pl.pallas_call(functools.partial(product_kernel, transpose, cap, n_out, l...  16.2 us
    unnamed x8, local copies, waits for them, and re-layouts  5.04 us
  transfers between devices with their start and end apart: 35, of which 16 were waited for; matrix products, arithmetic and copies ran while one was open for 5% of the time, Pallas kernels for 14%

profile of v1, /device:TPU:5, one launch (start us, length us, event | category | flops | bytes accessed | tf_op | source)
XLA Modules:
  0.0 114.3 jit_solution(352011543507051100)
XLA Ops:
  0.0 0.7 collective-permute-start.4
  0.7 0.9 reshape.25
  1.6 0.7 broadcast_in_dim.34
  3.2 0.7 pad_add_fusion
  3.8 0.4 collective-permute-start.3
  4.3 1.4 %collective-permute-start = (f32[4,40,128]{2,1,0:T(8,128)S(1)}, f32[4,40,128]{2,1,0:T(8,128)S(1)}, u32[]{:S(2)}, u32[]{:S(2)}) collective-permute-start(f32[4,40,128]{2,1,0:T(8,128)S(1)} %get-tuple-element.78), channel_id=1, source_target_pairs={{0,2},{1,3},{2,0},{3,1},{4,6},{5,7},{6,4},{7,5},{8,10},{9,11},{10,... | collective-permute-start | bytes 245768 | tf_op jit(solution)/shard_map/ppermute | solution.py:189
  5.7 0.8 compare_select_fusion.37
  6.5 1.1 collective-permute-done.3
  7.6 0.5 slice.106
  8.1 0.7 compare_select_fusion.35
  8.8 0.7 concatenate.50.meta_in
  9.7 2.4 %collective-permute-start.6 = (bf16[16,32,128]{2,1,0:T(8,128)(2,1)S(1)}, bf16[16,32,128]{2,1,0:T(8,128)(2,1)S(1)}, u32[]{:S(2)}, u32[]{:S(2)}) collective-permute-start(bf16[16,32,128]{2,1,0:T(8,128)(2,1)S(1)} %multiply_convert_fusion.2.vecs_in), channel_id=1, source_target_pairs={{0,16},{1,17},{2,18},{3,19},{4,20},{5,21},{6,22},{7,23},{8,24},{9,... | collective-permute-start | bytes 393224 | tf_op jit(solution)/shard_map/ppermute | solution.py:189
  12.1 2.2 %copy-done = bf16[1,1,128,128,128]{4,3,2,1,0:T(8,128)(2,1)S(1)} copy-done((bf16[1,1,128,128,128]{4,3,2,1,0:T(8,128)(2,1)S(1)}, bf16[1,1,128,128,128]{4,3,2,1,0:T(8,128)(2,1)}, u32[]{:S(2)}) %copy-start) | copy-done | bytes 4194328
  14.3 2.7 %transposed.3 = (f32[16,32,128]{2,1,0:T(8,128)S(1)}, f32[16,32,128]{2,1,0:T(8,128)S(1)}, bf16[16,32,128]{2,1,0:T(8,128)(2,1)S(1)}, bf16[16,32,128]{2,1,0:T(8,128)(2,1)S(1)}) custom-call(s32[1152]{0:T(1024)S(1)} %concatenate.50.meta_in, bf16[16,32,128]{2,1,0:T(8,128)(2,1)S(1)} %multiply_convert_fusion.2.vecs_in, bf16[128,128,128]{2,1,0:T(8,128)(2,1)S(1)} %bitcast.67, ...), custom_call_target="tpu_custom_call" | custom-call | flops 268435456 | bytes 655360 | tf_op jit(solution)/shard_map/transposed/pallas_call | solution.py:152
  17.0 1.2 %collective-permute-done.6 = bf16[16,32,128]{2,1,0:T(8,128)(2,1)S(1)} collective-permute-done((bf16[16,32,128]{2,1,0:T(8,128)(2,1)S(1)}, bf16[16,32,128]{2,1,0:T(8,128)(2,1)S(1)}, u32[]{:S(2)}, u32[]{:S(2)}) %collective-permute-start.6) | collective-permute-done | bytes 131104 | tf_op jit(solution)/shard_map/ppermute | solution.py:189
  18.2 1.2 %collective-permute-start.7 = (bf16[16,32,128]{2,1,0:T(8,128)(2,1)S(1)}, bf16[16,32,128]{2,1,0:T(8,128)(2,1)S(1)}, u32[]{:S(2)}, u32[]{:S(2)}) collective-permute-start(bf16[16,32,128]{2,1,0:T(8,128)(2,1)S(1)} %maximum_select_fusion.1), channel_id=1, source_target_pairs={{0,8},{1,9},{2,10},{3,11},{4,12},{5,13},{6,14},{7,15},{8,0},{9,1},... | collective-permute-start | bytes 393224 | tf_op jit(solution)/shard_map/ppermute | solution.py:189
  19.5 1.3 %collective-permute-start.9 = (bf16[16,32,128]{2,1,0:T(8,128)(2,1)S(1)}, bf16[16,32,128]{2,1,0:T(8,128)(2,1)S(1)}, u32[]{:S(2)}, u32[]{:S(2)}) collective-permute-start(bf16[16,32,128]{2,1,0:T(8,128)(2,1)S(1)} %maximum_select_fusion.1), channel_id=1, source_target_pairs={{0,12},{1,13},{2,14},{3,15},{4,8},{5,9},{6,10},{7,11},{8,4},{9,5},... | collective-permute-start | bytes 393224 | tf_op jit(solution)/shard_map/ppermute | solution.py:189
  20.8 0.3 collective-permute-start.8
  21.1 1.0 collective-permute-done.7
  22.1 3.8 %collective-permute-start.10 = (bf16[16,48,128]{2,1,0:T(8,128)(2,1)S(1)}, bf16[16,48,128]{2,1,0:T(8,128)(2,1)S(1)}, u32[]{:S(2)}, u32[]{:S(2)}) collective-permute-start(bf16[16,48,128]{2,1,0:T(8,128)(2,1)S(1)} %pad_maximum_fusion.4), channel_id=1, source_target_pairs={{0,16},{1,17},{2,18},{3,19},{4,20},{5,21},{6,22},{7,23},{8,24},{9,... | collective-permute-start | bytes 589832 | tf_op jit(solution)/shard_map/ppermute | solution.py:189
  26.0 1.2 %collective-permute-start.5 = (bf16[16,32,128]{2,1,0:T(8,128)(2,1)S(1)}, bf16[16,32,128]{2,1,0:T(8,128)(2,1)S(1)}, u32[]{:S(2)}, u32[]{:S(2)}) collective-permute-start(bf16[16,32,128]{2,1,0:T(8,128)(2,1)S(1)} %get-tuple-element.42.refs_3_), channel_id=1, source_target_pairs={{0,4},{1,5},{2,6},{3,7},{4,0},{5,1},{6,2},{7,3},{8,12},{9,13},{10,... | collective-permute-start | bytes 393224 | tf_op jit(solution)/shard_map/ppermute | solution.py:189
  27.2 0.3 collective-permute-start.11
  27.4 0.4 collective-permute-done.8
  27.9 2.2 %copy-done.1 = bf16[1,1,128,128,128]{4,3,2,1,0:T(8,128)(2,1)S(1)} copy-done((bf16[1,1,128,128,128]{4,3,2,1,0:T(8,128)(2,1)S(1)}, bf16[1,1,128,128,128]{4,3,2,1,0:T(8,128)(2,1)}, u32[]{:S(2)}) %copy-start.1) | copy-done | bytes 4194328
  30.1 2.7 %direct.3 = bf16[16,32,128]{2,1,0:T(8,128)(2,1)S(1)} custom-call(s32[1152]{0:T(1024)S(1)} %concatenate.50.meta_in, bf16[64,32,128]{2,1,0:T(8,128)(2,1)S(1)} %pad_maximum_fusion.vecs_in, bf16[128,128,128]{2,1,0:T(8,128)(2,1)S(1)} %bitcast.68, bf16[128,128,128]{2,1,0:T(8,128)(2,1)} %collective-permute-done.4.refs_1_, ...), custom_call_target="tpu_custom_call" | custom-call | flops 268435456 | bytes 655360 | tf_op jit(solution)/shard_map/direct/pallas_call | solution.py:152
  32.8 1.1 collective-permute-done.10
  34.1 2.0 %collective-permute-start.12 = (bf16[16,32,128]{2,1,0:T(8,128)(2,1)S(1)}, bf16[16,32,128]{2,1,0:T(8,128)(2,1)S(1)}, u32[]{:S(2)}, u32[]{:S(2)}) collective-permute-start(bf16[16,32,128]{2,1,0:T(8,128)(2,1)S(1)} %add_convert_fusion.2), channel_id=1, source_target_pairs={{0,8},{1,9},{2,10},{3,11},{4,12},{5,13},{6,14},{7,15},{8,0},{9,1},... | collective-permute-start | bytes 393224 | tf_op jit(solution)/shard_map/ppermute | solution.py:189
  36.1 0.2 collective-permute-start.13
  36.3 2.1 %collective-permute-done.12 = bf16[16,32,128]{2,1,0:T(8,128)(2,1)S(1)} collective-permute-done((bf16[16,32,128]{2,1,0:T(8,128)(2,1)S(1)}, bf16[16,32,128]{2,1,0:T(8,128)(2,1)S(1)}, u32[]{:S(2)}, u32[]{:S(2)}) %collective-permute-start.12) | collective-permute-done | bytes 131104 | tf_op jit(solution)/shard_map/ppermute | solution.py:189
  38.5 1.8 %collective-permute-done.13 = bf16[16,32,128]{2,1,0:T(8,128)(2,1)S(1)} collective-permute-done((bf16[16,32,128]{2,1,0:T(8,128)(2,1)S(1)}, bf16[16,32,128]{2,1,0:T(8,128)(2,1)S(1)}, u32[]{:S(2)}, u32[]{:S(2)}) %collective-permute-start.13) | collective-permute-done | bytes 131104 | tf_op jit(solution)/shard_map/ppermute | solution.py:189
  40.2 0.1 fusion.34
  40.3 3.2 %collective-permute-start.14 = (bf16[16,32,128]{2,1,0:T(8,128)(2,1)S(1)}, bf16[16,32,128]{2,1,0:T(8,128)(2,1)S(1)}, u32[]{:S(2)}, u32[]{:S(2)}) collective-permute-start(bf16[16,32,128]{2,1,0:T(8,128)(2,1)S(1)} %get-tuple-element.63), channel_id=1, source_target_pairs={{0,16},{1,17},{2,18},{3,19},{4,20},{5,21},{6,22},{7,23},{8,24},{9,... | collective-permute-start | bytes 393224 | tf_op jit(solution)/shard_map/ppermute | solution.py:189
  43.5 6.0 %collective-permute-done.14 = bf16[16,32,128]{2,1,0:T(8,128)(2,1)S(1)} collective-permute-done((bf16[16,32,128]{2,1,0:T(8,128)(2,1)S(1)}, bf16[16,32,128]{2,1,0:T(8,128)(2,1)S(1)}, u32[]{:S(2)}, u32[]{:S(2)}) %collective-permute-start.14) | collective-permute-done | bytes 131104 | tf_op jit(solution)/shard_map/ppermute | solution.py:189
  49.4 0.1 multiply_convert_fusion.1
  49.7 1.7 %collective-permute-start.20 = (bf16[16,32,128]{2,1,0:T(8,128)(2,1)S(1)}, bf16[16,32,128]{2,1,0:T(8,128)(2,1)S(1)}, u32[]{:S(2)}, u32[]{:S(2)}) collective-permute-start(bf16[16,32,128]{2,1,0:T(8,128)(2,1)S(1)} %get-tuple-element.61), channel_id=1, source_target_pairs={{0,4},{1,5},{2,6},{3,7},{4,0},{5,1},{6,2},{7,3},{8,12},{9,13},{10,... | collective-permute-start | bytes 393224 | tf_op jit(solution)/shard_map/ppermute | solution.py:189
  51.4 1.1 collective-permute-start.19
  52.5 0.9 collective-permute-done.15
  53.4 2.7 %transposed.4 = (f32[16,32,128]{2,1,0:T(8,128)S(1)}, f32[16,32,128]{2,1,0:T(8,128)S(1)}, bf16[16,32,128]{2,1,0:T(8,128)(2,1)S(1)}, bf16[16,32,128]{2,1,0:T(8,128)(2,1)S(1)}) custom-call(s32[1152]{0:T(1024)S(1)} %concatenate.50.meta_in, bf16[16,32,128]{2,1,0:T(8,128)(2,1)S(1)} %broadcast_select_fusion.1.vecs_in, bf16[128,128,128]{2,1,0:T(8,128)(2,1)S(1)} %bitcast.69, ...), custom_call_target="tpu_custom_call" | custom-call | flops 268435456 | bytes 655360 | tf_op jit(solution)/shard_map/transposed/pallas_call | solution.py:152
  56.1 1.8 %collective-permute-start.16 = (bf16[16,32,128]{2,1,0:T(8,128)(2,1)S(1)}, bf16[16,32,128]{2,1,0:T(8,128)(2,1)S(1)}, u32[]{:S(2)}, u32[]{:S(2)}) collective-permute-start(bf16[16,32,128]{2,1,0:T(8,128)(2,1)S(1)} %get-tuple-element.50.refs_2_), channel_id=1, source_target_pairs={{0,4},{1,5},{2,6},{3,7},{4,0},{5,1},{6,2},{7,3},{8,12},{9,13},{10,... | collective-permute-start | bytes 393224 | tf_op jit(solution)/shard_map/ppermute | solution.py:189
  58.1 2.7 %direct.4 = bf16[16,32,128]{2,1,0:T(8,128)(2,1)S(1)} custom-call(s32[1152]{0:T(1024)S(1)} %concatenate.50.meta_in, bf16[64,32,128]{2,1,0:T(8,128)(2,1)S(1)} %pad_maximum_fusion.1.vecs_in, bf16[128,128,128]{2,1,0:T(8,128)(2,1)S(1)} %bitcast.70, bf16[128,128,128]{2,1,0:T(8,128)(2,1)} %collective-permute-done.4.refs_1_, ...), custom_call_target="tpu_custom_call" | custom-call | flops 268435456 | bytes 655360 | tf_op jit(solution)/shard_map/direct/pallas_call | solution.py:152
  60.8 1.2 %collective-permute-start.22 = (bf16[16,32,128]{2,1,0:T(8,128)(2,1)S(1)}, bf16[16,32,128]{2,1,0:T(8,128)(2,1)S(1)}, u32[]{:S(2)}, u32[]{:S(2)}) collective-permute-start(bf16[16,32,128]{2,1,0:T(8,128)(2,1)S(1)} %direct.4), channel_id=1, source_target_pairs={{0,2},{1,3},{2,0},{3,1},{4,6},{5,7},{6,4},{7,5},{8,10},{9,11},{10,... | collective-permute-start | bytes 393224 | tf_op jit(solution)/shard_map/ppermute | solution.py:189
  62.0 1.7 %collective-permute-start.18 = (bf16[16,32,128]{2,1,0:T(8,128)(2,1)S(1)}, bf16[16,32,128]{2,1,0:T(8,128)(2,1)S(1)}, u32[]{:S(2)}, u32[]{:S(2)}) collective-permute-start(bf16[16,32,128]{2,1,0:T(8,128)(2,1)S(1)} %add_convert_fusion.1), channel_id=1, source_target_pairs={{0,8},{1,9},{2,10},{3,11},{4,12},{5,13},{6,14},{7,15},{8,0},{9,1},... | collective-permute-start | bytes 393224 | tf_op jit(solution)/shard_map/ppermute | solution.py:189
  63.7 1.3 %collective-permute-done.22 = bf16[16,32,128]{2,1,0:T(8,128)(2,1)S(1)} collective-permute-done((bf16[16,32,128]{2,1,0:T(8,128)(2,1)S(1)}, bf16[16,32,128]{2,1,0:T(8,128)(2,1)S(1)}, u32[]{:S(2)}, u32[]{:S(2)}) %collective-permute-start.22) | collective-permute-done | bytes 131104 | tf_op jit(solution)/shard_map/ppermute | solution.py:189
  65.0 1.1 collective-permute-done.18
  66.1 0.1 fusion.33
  66.2 2.3 %collective-permute-start.23 = (bf16[16,32,128]{2,1,0:T(8,128)(2,1)S(1)}, bf16[16,32,128]{2,1,0:T(8,128)(2,1)S(1)}, u32[]{:S(2)}, u32[]{:S(2)}) collective-permute-start(bf16[16,32,128]{2,1,0:T(8,128)(2,1)S(1)} %get-tuple-element.59), channel_id=1, source_target_pairs={{0,16},{1,17},{2,18},{3,19},{4,20},{5,21},{6,22},{7,23},{8,24},{9,... | collective-permute-start | bytes 393224 | tf_op jit(solution)/shard_map/ppermute | solution.py:189
  68.4 2.6 %collective-permute-done.23 = bf16[16,32,128]{2,1,0:T(8,128)(2,1)S(1)} collective-permute-done((bf16[16,32,128]{2,1,0:T(8,128)(2,1)S(1)}, bf16[16,32,128]{2,1,0:T(8,128)(2,1)S(1)}, u32[]{:S(2)}, u32[]{:S(2)}) %collective-permute-start.23) | collective-permute-done | bytes 131104 | tf_op jit(solution)/shard_map/ppermute | solution.py:189
  71.1 0.1 multiply_convert_fusion
  71.2 2.9 %collective-permute-start.24 = (bf16[16,32,128]{2,1,0:T(8,128)(2,1)S(1)}, bf16[16,32,128]{2,1,0:T(8,128)(2,1)S(1)}, u32[]{:S(2)}, u32[]{:S(2)}) collective-permute-start(bf16[16,32,128]{2,1,0:T(8,128)(2,1)S(1)} %get-tuple-element.57), channel_id=1, source_target_pairs={{0,2},{1,3},{2,0},{3,1},{4,6},{5,7},{6,4},{7,5},{8,10},{9,11},{10,... | collective-permute-start | bytes 393224 | tf_op jit(solution)/shard_map/ppermute | solution.py:189
  74.1 1.0 collective-permute-start.29
  75.1 1.6 %collective-permute-start.28 = (bf16[16,32,128]{2,1,0:T(8,128)(2,1)S(1)}, bf16[16,32,128]{2,1,0:T(8,128)(2,1)S(1)}, u32[]{:S(2)}, u32[]{:S(2)}) collective-permute-start(bf16[16,32,128]{2,1,0:T(8,128)(2,1)S(1)} %get-tuple-element.57), channel_id=1, source_target_pairs={{0,8},{1,9},{2,10},{3,11},{4,12},{5,13},{6,14},{7,15},{8,0},{9,1},... | collective-permute-start | bytes 393224 | tf_op jit(solution)/shard_map/ppermute | solution.py:189
  76.8 2.7 %transposed.5 = (f32[16,32,128]{2,1,0:T(8,128)S(1)}, f32[16,32,128]{2,1,0:T(8,128)S(1)}, bf16[16,32,128]{2,1,0:T(8,128)(2,1)S(1)}, bf16[16,32,128]{2,1,0:T(8,128)(2,1)S(1)}) custom-call(s32[1152]{0:T(1024)S(1)} %concatenate.50.meta_in, bf16[16,32,128]{2,1,0:T(8,128)(2,1)S(1)} %broadcast_select_fusion.vecs_in, bf16[128,128,128]{2,1,0:T(8,128)(2,1)S(1)} %bitcast.71, ...), custom_call_target="tpu_custom_call" | custom-call | flops 268435456 | bytes 655360 | tf_op jit(solution)/shard_map/transposed/pallas_call | solution.py:152
  79.5 0.8 collective-permute-start.25
  80.3 0.7 collective-permute-start.26
  81.1 2.7 %direct.5 = bf16[16,32,128]{2,1,0:T(8,128)(2,1)S(1)} custom-call(s32[1152]{0:T(1024)S(1)} %concatenate.50.meta_in, bf16[64,32,128]{2,1,0:T(8,128)(2,1)S(1)} %pad_maximum_fusion.2.vecs_in, bf16[128,128,128]{2,1,0:T(8,128)(2,1)S(1)} %bitcast.72, bf16[128,128,128]{2,1,0:T(8,128)(2,1)} %collective-permute-done.4.refs_1_, ...), custom_call_target="tpu_custom_call" | custom-call | flops 268435456 | bytes 655360 | tf_op jit(solution)/shard_map/direct/pallas_call | solution.py:152
  83.8 1.2 %collective-permute-start.31 = (bf16[16,32,128]{2,1,0:T(8,128)(2,1)S(1)}, bf16[16,32,128]{2,1,0:T(8,128)(2,1)S(1)}, u32[]{:S(2)}, u32[]{:S(2)}) collective-permute-start(bf16[16,32,128]{2,1,0:T(8,128)(2,1)S(1)} %direct.5), channel_id=1, source_target_pairs={{0,2},{1,3},{2,0},{3,1},{4,6},{5,7},{6,4},{7,5},{8,10},{9,11},{10,... | collective-permute-start | bytes 393224 | tf_op jit(solution)/shard_map/ppermute | solution.py:189
  85.0 2.6 %collective-permute-done.26 = bf16[16,32,128]{2,1,0:T(8,128)(2,1)S(1)} collective-permute-done((bf16[16,32,128]{2,1,0:T(8,128)(2,1)S(1)}, bf16[16,32,128]{2,1,0:T(8,128)(2,1)S(1)}, u32[]{:S(2)}, u32[]{:S(2)}) %collective-permute-start.26) | collective-permute-done | bytes 131104 | tf_op jit(solution)/shard_map/ppermute | solution.py:189
  87.7 4.1 %collective-permute-done.27 = bf16[16,32,128]{2,1,0:T(8,128)(2,1)S(1)} collective-permute-done((bf16[16,32,128]{2,1,0:T(8,128)(2,1)S(1)}, bf16[16,32,128]{2,1,0:T(8,128)(2,1)S(1)}, u32[]{:S(2)}, u32[]{:S(2)}) %collective-permute-start.27) | collective-permute-done | bytes 131104 | tf_op jit(solution)/shard_map/ppermute | solution.py:189
  91.9 1.2 %collective-permute-start.32 = (bf16[8,32,128]{2,1,0:T(8,128)(2,1)S(1)}, bf16[8,32,128]{2,1,0:T(8,128)(2,1)S(1)}, u32[]{:S(2)}, u32[]{:S(2)}) collective-permute-start(bf16[8,32,128]{2,1,0:T(8,128)(2,1)S(1)} %slice.200), channel_id=1, source_target_pairs={{0,16},{1,17},{2,18},{3,19},{4,20},{5,21},{6,22},{7,23},{8,24},{9,... | collective-permute-start | bytes 196616 | tf_op jit(solution)/shard_map/ppermute | solution.py:189
  93.1 3.3 %collective-permute-done.32 = bf16[8,32,128]{2,1,0:T(8,128)(2,1)S(1)} collective-permute-done((bf16[8,32,128]{2,1,0:T(8,128)(2,1)S(1)}, bf16[8,32,128]{2,1,0:T(8,128)(2,1)S(1)}, u32[]{:S(2)}, u32[]{:S(2)}) %collective-permute-start.32) | collective-permute-done | bytes 65568 | tf_op jit(solution)/shard_map/ppermute | solution.py:189
  96.5 7.8 %collective-permute-start.34 = (f32[4,32,128]{2,1,0:T(8,128)S(1)}, f32[4,32,128]{2,1,0:T(8,128)S(1)}, u32[]{:S(2)}, u32[]{:S(2)}) collective-permute-start(f32[4,32,128]{2,1,0:T(8,128)S(1)} %get-tuple-element.81), channel_id=1, source_target_pairs={{1,0},{0,1},{17,2},{16,3},{5,4},{4,5},{21,6},{20,7},{9,8},{8,9},{2... | collective-permute-start | bytes 196616 | tf_op jit(solution)/shard_map/ppermute | solution.py:189
  104.2 2.3 %collective-permute-start.33 = (f32[4,32,128]{2,1,0:T(8,128)S(1)}, f32[4,32,128]{2,1,0:T(8,128)S(1)}, u32[]{:S(2)}, u32[]{:S(2)}) collective-permute-start(f32[4,32,128]{2,1,0:T(8,128)S(1)} %get-tuple-element.82), channel_id=1, source_target_pairs={{0,0},{1,1},{16,2},{17,3},{4,4},{5,5},{20,6},{21,7},{8,8},{9,9},{2... | collective-permute-start | bytes 196616 | tf_op jit(solution)/shard_map/ppermute | solution.py:189
  106.6 6.9 %collective-permute-done.33 = f32[4,32,128]{2,1,0:T(8,128)S(1)} collective-permute-done((f32[4,32,128]{2,1,0:T(8,128)S(1)}, f32[4,32,128]{2,1,0:T(8,128)S(1)}, u32[]{:S(2)}, u32[]{:S(2)}) %collective-permute-start.33) | collective-permute-done | bytes 65568 | tf_op jit(solution)/shard_map/ppermute | solution.py:189
  113.7 0.7 copy.15
  (72 shorter events, 1.5 us)
Async XLA Ops:
  0.0 9.6 %collective-permute-start.4 = (bf16[128,128,128]{2,1,0:T(8,128)(2,1)}, bf16[128,128,128]{2,1,0:T(8,128)(2,1)}, u32[]{:S(2)}, u32[]{:S(2)}) collective-permute-start(bf16[128,128,128]{2,1,0:T(8,128)(2,1)} %bitcast.66), channel_id=1, source_target_pairs={{0,1},{1,0},{2,3},{3,2},{4,5},{5,4},{6,7},{7,6},{8,9},{9,8},{10,11... | collective-permute-start | bytes 12582920 | tf_op jit(solution)/shard_map/ppermute | solution.py:189
  2.4 7.2 %collective-permute-start.2 = (f32[4,40,128]{2,1,0:T(8,128)S(1)}, f32[4,40,128]{2,1,0:T(8,128)S(1)}, u32[]{:S(2)}, u32[]{:S(2)}) collective-permute-start(f32[4,40,128]{2,1,0:T(8,128)S(1)} %get-tuple-element.77), channel_id=1, source_target_pairs={{0,1},{1,0},{2,3},{3,2},{4,5},{5,4},{6,7},{7,6},{8,9},{9,8},{10,11... | collective-permute-start | bytes 245768 | tf_op jit(solution)/shard_map/ppermute | solution.py:189
  2.4 7.1 %collective-permute-start.1 = (f32[4,40,128]{2,1,0:T(8,128)S(1)}, f32[4,40,128]{2,1,0:T(8,128)S(1)}, u32[]{:S(2)}, u32[]{:S(2)}) collective-permute-start(f32[4,40,128]{2,1,0:T(8,128)S(1)} %get-tuple-element.77), channel_id=1, source_target_pairs={{0,3},{1,2},{2,1},{3,0},{4,7},{5,6},{6,5},{7,4},{8,11},{9,10},{10,... | collective-permute-start | bytes 245768 | tf_op jit(solution)/shard_map/ppermute | solution.py:189
  3.8 3.7 %collective-permute-start.3 = (s32[257]{0:T(512)S(1)}, s32[257]{0:T(512)S(1)}, u32[]{:S(2)}, u32[]{:S(2)}) collective-permute-start(s32[257]{0:T(512)S(1)} %pad_add_fusion), channel_id=1, source_target_pairs={{0,1},{1,0},{2,3},{3,2},{4,5},{5,4},{6,7},{7,6},{8,9},{9,8},{10,11... | collective-permute-start | bytes 3092 | tf_op jit(solution)/shard_map/ppermute | solution.py:189
  4.3 5.3 %collective-permute-start = (f32[4,40,128]{2,1,0:T(8,128)S(1)}, f32[4,40,128]{2,1,0:T(8,128)S(1)}, u32[]{:S(2)}, u32[]{:S(2)}) collective-permute-start(f32[4,40,128]{2,1,0:T(8,128)S(1)} %get-tuple-element.78), channel_id=1, source_target_pairs={{0,2},{1,3},{2,0},{3,1},{4,6},{5,7},{6,4},{7,5},{8,10},{9,11},{10,... | collective-permute-start | bytes 245768 | tf_op jit(solution)/shard_map/ppermute | solution.py:189
  9.7 8.5 %collective-permute-start.6 = (bf16[16,32,128]{2,1,0:T(8,128)(2,1)S(1)}, bf16[16,32,128]{2,1,0:T(8,128)(2,1)S(1)}, u32[]{:S(2)}, u32[]{:S(2)}) collective-permute-start(bf16[16,32,128]{2,1,0:T(8,128)(2,1)S(1)} %multiply_convert_fusion.2.vecs_in), channel_id=1, source_target_pairs={{0,16},{1,17},{2,18},{3,19},{4,20},{5,21},{6,22},{7,23},{8,24},{9,... | collective-permute-start | bytes 393224 | tf_op jit(solution)/shard_map/ppermute | solution.py:189
  12.1 2.2 %copy-start = (bf16[1,1,128,128,128]{4,3,2,1,0:T(8,128)(2,1)S(1)}, bf16[1,1,128,128,128]{4,3,2,1,0:T(8,128)(2,1)}, u32[]{:S(2)}) copy-start(bf16[1,1,128,128,128]{4,3,2,1,0:T(8,128)(2,1)} %param.7) | copy-start | bytes 12582916
  18.2 3.9 %collective-permute-start.7 = (bf16[16,32,128]{2,1,0:T(8,128)(2,1)S(1)}, bf16[16,32,128]{2,1,0:T(8,128)(2,1)S(1)}, u32[]{:S(2)}, u32[]{:S(2)}) collective-permute-start(bf16[16,32,128]{2,1,0:T(8,128)(2,1)S(1)} %maximum_select_fusion.1), channel_id=1, source_target_pairs={{0,8},{1,9},{2,10},{3,11},{4,12},{5,13},{6,14},{7,15},{8,0},{9,1},... | collective-permute-start | bytes 393224 | tf_op jit(solution)/shard_map/ppermute | solution.py:189
  19.5 8.0 %collective-permute-start.9 = (bf16[16,32,128]{2,1,0:T(8,128)(2,1)S(1)}, bf16[16,32,128]{2,1,0:T(8,128)(2,1)S(1)}, u32[]{:S(2)}, u32[]{:S(2)}) collective-permute-start(bf16[16,32,128]{2,1,0:T(8,128)(2,1)S(1)} %maximum_select_fusion.1), channel_id=1, source_target_pairs={{0,12},{1,13},{2,14},{3,15},{4,8},{5,9},{6,10},{7,11},{8,4},{9,5},... | collective-permute-start | bytes 393224 | tf_op jit(solution)/shard_map/ppermute | solution.py:189
  20.8 7.0 %collective-permute-start.8 = (bf16[16,32,128]{2,1,0:T(8,128)(2,1)S(1)}, bf16[16,32,128]{2,1,0:T(8,128)(2,1)S(1)}, u32[]{:S(2)}, u32[]{:S(2)}) collective-permute-start(bf16[16,32,128]{2,1,0:T(8,128)(2,1)S(1)} %maximum_select_fusion.1), channel_id=1, source_target_pairs={{0,4},{1,5},{2,6},{3,7},{4,0},{5,1},{6,2},{7,3},{8,12},{9,13},{10,... | collective-permute-start | bytes 393224 | tf_op jit(solution)/shard_map/ppermute | solution.py:189
  22.1 11.8 %collective-permute-start.10 = (bf16[16,48,128]{2,1,0:T(8,128)(2,1)S(1)}, bf16[16,48,128]{2,1,0:T(8,128)(2,1)S(1)}, u32[]{:S(2)}, u32[]{:S(2)}) collective-permute-start(bf16[16,48,128]{2,1,0:T(8,128)(2,1)S(1)} %pad_maximum_fusion.4), channel_id=1, source_target_pairs={{0,16},{1,17},{2,18},{3,19},{4,20},{5,21},{6,22},{7,23},{8,24},{9,... | collective-permute-start | bytes 589832 | tf_op jit(solution)/shard_map/ppermute | solution.py:189
  26.0 6.9 %collective-permute-start.5 = (bf16[16,32,128]{2,1,0:T(8,128)(2,1)S(1)}, bf16[16,32,128]{2,1,0:T(8,128)(2,1)S(1)}, u32[]{:S(2)}, u32[]{:S(2)}) collective-permute-start(bf16[16,32,128]{2,1,0:T(8,128)(2,1)S(1)} %get-tuple-element.42.refs_3_), channel_id=1, source_target_pairs={{0,4},{1,5},{2,6},{3,7},{4,0},{5,1},{6,2},{7,3},{8,12},{9,13},{10,... | collective-permute-start | bytes 393224 | tf_op jit(solution)/shard_map/ppermute | solution.py:189
  27.2 9.1 %collective-permute-start.11 = (bf16[16,32,128]{2,1,0:T(8,128)(2,1)S(1)}, bf16[16,32,128]{2,1,0:T(8,128)(2,1)S(1)}, u32[]{:S(2)}, u32[]{:S(2)}) collective-permute-start(bf16[16,32,128]{2,1,0:T(8,128)(2,1)S(1)} %get-tuple-element.41.refs_2_), channel_id=1, source_target_pairs={{0,4},{1,5},{2,6},{3,7},{4,0},{5,1},{6,2},{7,3},{8,12},{9,13},{10,... | collective-permute-start | bytes 393224 | tf_op jit(solution)/shard_map/ppermute | solution.py:189
  27.9 2.2 %copy-start.1 = (bf16[1,1,128,128,128]{4,3,2,1,0:T(8,128)(2,1)S(1)}, bf16[1,1,128,128,128]{4,3,2,1,0:T(8,128)(2,1)}, u32[]{:S(2)}) copy-start(bf16[1,1,128,128,128]{4,3,2,1,0:T(8,128)(2,1)} %param.7) | copy-start | bytes 12582916
  34.1 4.4 %collective-permute-start.12 = (bf16[16,32,128]{2,1,0:T(8,128)(2,1)S(1)}, bf16[16,32,128]{2,1,0:T(8,128)(2,1)S(1)}, u32[]{:S(2)}, u32[]{:S(2)}) collective-permute-start(bf16[16,32,128]{2,1,0:T(8,128)(2,1)S(1)} %add_convert_fusion.2), channel_id=1, source_target_pairs={{0,8},{1,9},{2,10},{3,11},{4,12},{5,13},{6,14},{7,15},{8,0},{9,1},... | collective-permute-start | bytes 393224 | tf_op jit(solution)/shard_map/ppermute | solution.py:189
  36.1 4.1 %collective-permute-start.13 = (bf16[16,32,128]{2,1,0:T(8,128)(2,1)S(1)}, bf16[16,32,128]{2,1,0:T(8,128)(2,1)S(1)}, u32[]{:S(2)}, u32[]{:S(2)}) collective-permute-start(bf16[16,32,128]{2,1,0:T(8,128)(2,1)S(1)} %direct.3), channel_id=1, source_target_pairs={{0,2},{1,3},{2,0},{3,1},{4,6},{5,7},{6,4},{7,5},{8,10},{9,11},{10,... | collective-permute-start | bytes 393224 | tf_op jit(solution)/shard_map/ppermute | solution.py:189
  40.3 9.1 %collective-permute-start.14 = (bf16[16,32,128]{2,1,0:T(8,128)(2,1)S(1)}, bf16[16,32,128]{2,1,0:T(8,128)(2,1)S(1)}, u32[]{:S(2)}, u32[]{:S(2)}) collective-permute-start(bf16[16,32,128]{2,1,0:T(8,128)(2,1)S(1)} %get-tuple-element.63), channel_id=1, source_target_pairs={{0,16},{1,17},{2,18},{3,19},{4,20},{5,21},{6,22},{7,23},{8,24},{9,... | collective-permute-start | bytes 393224 | tf_op jit(solution)/shard_map/ppermute | solution.py:189
  49.5 3.9 %collective-permute-start.15 = (bf16[16,32,128]{2,1,0:T(8,128)(2,1)S(1)}, bf16[16,32,128]{2,1,0:T(8,128)(2,1)S(1)}, u32[]{:S(2)}, u32[]{:S(2)}) collective-permute-start(bf16[16,32,128]{2,1,0:T(8,128)(2,1)S(1)} %get-tuple-element.61), channel_id=1, source_target_pairs={{0,2},{1,3},{2,0},{3,1},{4,6},{5,7},{6,4},{7,5},{8,10},{9,11},{10,... | collective-permute-start | bytes 393224 | tf_op jit(solution)/shard_map/ppermute | solution.py:189
  49.6 8.3 %collective-permute-start.21 = (bf16[16,32,128]{2,1,0:T(8,128)(2,1)S(1)}, bf16[16,32,128]{2,1,0:T(8,128)(2,1)S(1)}, u32[]{:S(2)}, u32[]{:S(2)}) collective-permute-start(bf16[16,32,128]{2,1,0:T(8,128)(2,1)S(1)} %get-tuple-element.61), channel_id=1, source_target_pairs={{0,12},{1,13},{2,14},{3,15},{4,8},{5,9},{6,10},{7,11},{8,4},{9,5},... | collective-permute-start | bytes 393224 | tf_op jit(solution)/shard_map/ppermute | solution.py:189
  49.7 8.3 %collective-permute-start.20 = (bf16[16,32,128]{2,1,0:T(8,128)(2,1)S(1)}, bf16[16,32,128]{2,1,0:T(8,128)(2,1)S(1)}, u32[]{:S(2)}, u32[]{:S(2)}) collective-permute-start(bf16[16,32,128]{2,1,0:T(8,128)(2,1)S(1)} %get-tuple-element.61), channel_id=1, source_target_pairs={{0,4},{1,5},{2,6},{3,7},{4,0},{5,1},{6,2},{7,3},{8,12},{9,13},{10,... | collective-permute-start | bytes 393224 | tf_op jit(solution)/shard_map/ppermute | solution.py:189
  51.4 6.6 %collective-permute-start.19 = (bf16[16,32,128]{2,1,0:T(8,128)(2,1)S(1)}, bf16[16,32,128]{2,1,0:T(8,128)(2,1)S(1)}, u32[]{:S(2)}, u32[]{:S(2)}) collective-permute-start(bf16[16,32,128]{2,1,0:T(8,128)(2,1)S(1)} %get-tuple-element.61), channel_id=1, source_target_pairs={{0,8},{1,9},{2,10},{3,11},{4,12},{5,13},{6,14},{7,15},{8,0},{9,1},... | collective-permute-start | bytes 393224 | tf_op jit(solution)/shard_map/ppermute | solution.py:189
  56.1 8.8 %collective-permute-start.16 = (bf16[16,32,128]{2,1,0:T(8,128)(2,1)S(1)}, bf16[16,32,128]{2,1,0:T(8,128)(2,1)S(1)}, u32[]{:S(2)}, u32[]{:S(2)}) collective-permute-start(bf16[16,32,128]{2,1,0:T(8,128)(2,1)S(1)} %get-tuple-element.50.refs_2_), channel_id=1, source_target_pairs={{0,4},{1,5},{2,6},{3,7},{4,0},{5,1},{6,2},{7,3},{8,12},{9,13},{10,... | collective-permute-start | bytes 393224 | tf_op jit(solution)/shard_map/ppermute | solution.py:189
  57.9 4.1 %collective-permute-start.17 = (bf16[16,32,128]{2,1,0:T(8,128)(2,1)S(1)}, bf16[16,32,128]{2,1,0:T(8,128)(2,1)S(1)}, u32[]{:S(2)}, u32[]{:S(2)}) collective-permute-start(bf16[16,32,128]{2,1,0:T(8,128)(2,1)S(1)} %get-tuple-element.52.refs_3_), channel_id=1, source_target_pairs={{0,4},{1,5},{2,6},{3,7},{4,0},{5,1},{6,2},{7,3},{8,12},{9,13},{10,... | collective-permute-start | bytes 393224 | tf_op jit(solution)/shard_map/ppermute | solution.py:189
  60.8 4.2 %collective-permute-start.22 = (bf16[16,32,128]{2,1,0:T(8,128)(2,1)S(1)}, bf16[16,32,128]{2,1,0:T(8,128)(2,1)S(1)}, u32[]{:S(2)}, u32[]{:S(2)}) collective-permute-start(bf16[16,32,128]{2,1,0:T(8,128)(2,1)S(1)} %direct.4), channel_id=1, source_target_pairs={{0,2},{1,3},{2,0},{3,1},{4,6},{5,7},{6,4},{7,5},{8,10},{9,11},{10,... | collective-permute-start | bytes 393224 | tf_op jit(solution)/shard_map/ppermute | solution.py:189
  62.0 4.1 %collective-permute-start.18 = (bf16[16,32,128]{2,1,0:T(8,128)(2,1)S(1)}, bf16[16,32,128]{2,1,0:T(8,128)(2,1)S(1)}, u32[]{:S(2)}, u32[]{:S(2)}) collective-permute-start(bf16[16,32,128]{2,1,0:T(8,128)(2,1)S(1)} %add_convert_fusion.1), channel_id=1, source_target_pairs={{0,8},{1,9},{2,10},{3,11},{4,12},{5,13},{6,14},{7,15},{8,0},{9,1},... | collective-permute-start | bytes 393224 | tf_op jit(solution)/shard_map/ppermute | solution.py:189
  66.2 4.9 %collective-permute-start.23 = (bf16[16,32,128]{2,1,0:T(8,128)(2,1)S(1)}, bf16[16,32,128]{2,1,0:T(8,128)(2,1)S(1)}, u32[]{:S(2)}, u32[]{:S(2)}) collective-permute-start(bf16[16,32,128]{2,1,0:T(8,128)(2,1)S(1)} %get-tuple-element.59), channel_id=1, source_target_pairs={{0,16},{1,17},{2,18},{3,19},{4,20},{5,21},{6,22},{7,23},{8,24},{9,... | collective-permute-start | bytes 393224 | tf_op jit(solution)/shard_map/ppermute | solution.py:189
  71.2 5.6 %collective-permute-start.24 = (bf16[16,32,128]{2,1,0:T(8,128)(2,1)S(1)}, bf16[16,32,128]{2,1,0:T(8,128)(2,1)S(1)}, u32[]{:S(2)}, u32[]{:S(2)}) collective-permute-start(bf16[16,32,128]{2,1,0:T(8,128)(2,1)S(1)} %get-tuple-element.57), channel_id=1, source_target_pairs={{0,2},{1,3},{2,0},{3,1},{4,6},{5,7},{6,4},{7,5},{8,10},{9,11},{10,... | collective-permute-start | bytes 393224 | tf_op jit(solution)/shard_map/ppermute | solution.py:189
  74.1 6.9 %collective-permute-start.30 = (bf16[16,32,128]{2,1,0:T(8,128)(2,1)S(1)}, bf16[16,32,128]{2,1,0:T(8,128)(2,1)S(1)}, u32[]{:S(2)}, u32[]{:S(2)}) collective-permute-start(bf16[16,32,128]{2,1,0:T(8,128)(2,1)S(1)} %get-tuple-element.57), channel_id=1, source_target_pairs={{0,12},{1,13},{2,14},{3,15},{4,8},{5,9},{6,10},{7,11},{8,4},{9,5},... | collective-permute-start | bytes 393224 | tf_op jit(solution)/shard_map/ppermute | solution.py:189
  74.1 6.9 %collective-permute-start.29 = (bf16[16,32,128]{2,1,0:T(8,128)(2,1)S(1)}, bf16[16,32,128]{2,1,0:T(8,128)(2,1)S(1)}, u32[]{:S(2)}, u32[]{:S(2)}) collective-permute-start(bf16[16,32,128]{2,1,0:T(8,128)(2,1)S(1)} %get-tuple-element.57), channel_id=1, source_target_pairs={{0,4},{1,5},{2,6},{3,7},{4,0},{5,1},{6,2},{7,3},{8,12},{9,13},{10,... | collective-permute-start | bytes 393224 | tf_op jit(solution)/shard_map/ppermute | solution.py:189
  75.1 5.9 %collective-permute-start.28 = (bf16[16,32,128]{2,1,0:T(8,128)(2,1)S(1)}, bf16[16,32,128]{2,1,0:T(8,128)(2,1)S(1)}, u32[]{:S(2)}, u32[]{:S(2)}) collective-permute-start(bf16[16,32,128]{2,1,0:T(8,128)(2,1)S(1)} %get-tuple-element.57), channel_id=1, source_target_pairs={{0,8},{1,9},{2,10},{3,11},{4,12},{5,13},{6,14},{7,15},{8,0},{9,1},... | collective-permute-start | bytes 393224 | tf_op jit(solution)/shard_map/ppermute | solution.py:189
  79.5 8.2 %collective-permute-start.25 = (bf16[16,32,128]{2,1,0:T(8,128)(2,1)S(1)}, bf16[16,32,128]{2,1,0:T(8,128)(2,1)S(1)}, u32[]{:S(2)}, u32[]{:S(2)}) collective-permute-start(bf16[16,32,128]{2,1,0:T(8,128)(2,1)S(1)} %get-tuple-element.54.refs_2_), channel_id=1, source_target_pairs={{0,4},{1,5},{2,6},{3,7},{4,0},{5,1},{6,2},{7,3},{8,12},{9,13},{10,... | collective-permute-start | bytes 393224 | tf_op jit(solution)/shard_map/ppermute | solution.py:189
  80.3 7.3 %collective-permute-start.26 = (bf16[16,32,128]{2,1,0:T(8,128)(2,1)S(1)}, bf16[16,32,128]{2,1,0:T(8,128)(2,1)S(1)}, u32[]{:S(2)}, u32[]{:S(2)}) collective-permute-start(bf16[16,32,128]{2,1,0:T(8,128)(2,1)S(1)} %get-tuple-element.56.refs_3_), channel_id=1, source_target_pairs={{0,4},{1,5},{2,6},{3,7},{4,0},{5,1},{6,2},{7,3},{8,12},{9,13},{10,... | collective-permute-start | bytes 393224 | tf_op jit(solution)/shard_map/ppermute | solution.py:189
  83.8 3.9 %collective-permute-start.31 = (bf16[16,32,128]{2,1,0:T(8,128)(2,1)S(1)}, bf16[16,32,128]{2,1,0:T(8,128)(2,1)S(1)}, u32[]{:S(2)}, u32[]{:S(2)}) collective-permute-start(bf16[16,32,128]{2,1,0:T(8,128)(2,1)S(1)} %direct.5), channel_id=1, source_target_pairs={{0,2},{1,3},{2,0},{3,1},{4,6},{5,7},{6,4},{7,5},{8,10},{9,11},{10,... | collective-permute-start | bytes 393224 | tf_op jit(solution)/shard_map/ppermute | solution.py:189
  87.6 4.2 %collective-permute-start.27 = (bf16[16,32,128]{2,1,0:T(8,128)(2,1)S(1)}, bf16[16,32,128]{2,1,0:T(8,128)(2,1)S(1)}, u32[]{:S(2)}, u32[]{:S(2)}) collective-permute-start(bf16[16,32,128]{2,1,0:T(8,128)(2,1)S(1)} %add_convert_fusion), channel_id=1, source_target_pairs={{0,8},{1,9},{2,10},{3,11},{4,12},{5,13},{6,14},{7,15},{8,0},{9,1},... | collective-permute-start | bytes 393224 | tf_op jit(solution)/shard_map/ppermute | solution.py:189
  91.9 4.5 %collective-permute-start.32 = (bf16[8,32,128]{2,1,0:T(8,128)(2,1)S(1)}, bf16[8,32,128]{2,1,0:T(8,128)(2,1)S(1)}, u32[]{:S(2)}, u32[]{:S(2)}) collective-permute-start(bf16[8,32,128]{2,1,0:T(8,128)(2,1)S(1)} %slice.200), channel_id=1, source_target_pairs={{0,16},{1,17},{2,18},{3,19},{4,20},{5,21},{6,22},{7,23},{8,24},{9,... | collective-permute-start | bytes 196616 | tf_op jit(solution)/shard_map/ppermute | solution.py:189
  96.5 10.1 %collective-permute-start.34 = (f32[4,32,128]{2,1,0:T(8,128)S(1)}, f32[4,32,128]{2,1,0:T(8,128)S(1)}, u32[]{:S(2)}, u32[]{:S(2)}) collective-permute-start(f32[4,32,128]{2,1,0:T(8,128)S(1)} %get-tuple-element.81), channel_id=1, source_target_pairs={{1,0},{0,1},{17,2},{16,3},{5,4},{4,5},{21,6},{20,7},{9,8},{8,9},{2... | collective-permute-start | bytes 196616 | tf_op jit(solution)/shard_map/ppermute | solution.py:189
  104.2 9.3 %collective-permute-start.33 = (f32[4,32,128]{2,1,0:T(8,128)S(1)}, f32[4,32,128]{2,1,0:T(8,128)S(1)}, u32[]{:S(2)}, u32[]{:S(2)}) collective-permute-start(f32[4,32,128]{2,1,0:T(8,128)S(1)} %get-tuple-element.82), channel_id=1, source_target_pairs={{0,0},{1,1},{16,2},{17,3},{4,4},{5,5},{20,6},{21,7},{8,8},{9,9},{2... | collective-permute-start | bytes 196616 | tf_op jit(solution)/shard_map/ppermute | solution.py:189

commit v2 on v0

--- a/solution.py
+++ b/solution.py
@@ -12,7 +12,8 @@
 center_shift = 0.5
 half_width = 3.0
 
-UNROLL = 64
+UNROLL_TRANSPOSED = 32
+UNROLL_DIRECT = 64
 PACK = 4
 VMEM_LIMIT = 16 * 1024 * 1024
 AXES = ("row", "col")
@@ -70,8 +71,8 @@
     return [(b, a) for a, b in pairs]
 
 
-def live_groups(meta_ref, cap, which):
-    return jnp.maximum((meta_ref[8 * cap + which] + (UNROLL - 1)) // UNROLL, 1)
+def live_groups(meta_ref, cap, which, unroll):
+    return jnp.maximum((meta_ref[8 * cap + which] + (unroll - 1)) // unroll, 1)
 
 
 def product_kernel(transpose, cap, n_out, after, meta_in, vecs_in, *refs):
@@ -79,11 +80,12 @@
     outs, refs = refs[:n_out], refs[n_out:]
     meta_ref, vecs_ref, slabs, acc, slab_sem, in_sem = refs
     base = 0 if transpose else 4 * cap
+    unroll = UNROLL_TRANSPOSED if transpose else UNROLL_DIRECT
 
     def slab_copy(which, g):
-        span = pl.ds(g * UNROLL, UNROLL)
-        to = pl.ds(which * cap + g * UNROLL, UNROLL)
-        sem = slab_sem.at[which * (cap // UNROLL) + g]
+        span = pl.ds(g * unroll, unroll)
+        to = pl.ds(which * cap + g * unroll, unroll)
+        sem = slab_sem.at[which * (cap // unroll) + g]
         return pltpu.make_async_copy(slab_refs[which].at[span], slabs.at[to], sem)
 
     def start_slab(which, g, carry):
@@ -98,7 +100,7 @@
     slab_copy(1, 0).start()
     acc[...] = jnp.zeros_like(acc)
     meta_copy.wait()
-    groups = [live_groups(meta_ref, cap, which) for which in range(2)]
+    groups = [live_groups(meta_ref, cap, which, unroll) for which in range(2)]
     for which in range(2):
         lax.fori_loop(1, groups[which], functools.partial(start_slab, which), 0)
     vecs_copy.wait()
@@ -107,9 +109,9 @@
 
     def body(which, g, carry):
         slab_copy(which, g).wait()
-        start = which * cap + g * UNROLL
+        start = which * cap + g * unroll
         products = []
-        for u in range(0, UNROLL, PACK):
+        for u in range(0, unroll, PACK):
             v = [vecs_ref[meta_ref[base + start + u + k]] for k in range(PACK)]
             m = [slabs[start + u + k] for k in range(PACK)]
             left = jnp.concatenate([
@@ -125,7 +127,7 @@
             products.append(
                 lax.dot_general(left, right, dims, preferred_element_type=jnp.float32)
             )
-        for u in range(UNROLL):
+        for u in range(unroll):
             k = u % PACK
             rows = slice(k * vec_count, (k + 1) * vec_count)
             lanes = slice((k // 2) * block_len, (k // 2 + 1) * block_len)
@@ -159,7 +161,7 @@
             pltpu.VMEM(vecs.shape, jnp.bfloat16),
             pltpu.VMEM((2 * cap, block_len, block_len), jnp.bfloat16),
             pltpu.VMEM((total_out + 1, vec_count, block_len), jnp.float32),
-            pltpu.SemaphoreType.DMA((2 * cap // UNROLL,)),
+            pltpu.SemaphoreType.DMA((2 * cap // min(UNROLL_TRANSPOSED, UNROLL_DIRECT),)),
             pltpu.SemaphoreType.DMA((2,)),
         ],
         compiler_params=pltpu.CompilerParams(vmem_limit_bytes=VMEM_LIMIT),

time: 115 us -> 114 us (level)
  waiting for transfers between devices: 38.2 us -> 32.1 us
  Pallas kernels: 16.1 us -> 20.3 us
    ppermute x35, waiting for transfers between devices: 38.2 us -> 32.1 us  [send(): return lax.ppermute(x, AXES, pairs)]
    pallas_call x6, Pallas kernels: 16.1 us -> 20.3 us  [products(): pl.pallas_call(functools.partial(product_kernel, transpose, cap, n_out, l...]
  transfers between devices with their start and end apart: 35 -> 35, of which waited for: 18 -> 17; matrix products, arithmetic and copies ran while one was open for 5% -> 5% of each run, Pallas kernels for 14% -> 18%
where the time goes in v2:
time: 114 us; the launch traced here: 113 us
  starting transfers between devices  48.4 us (42%)
  waiting for transfers between devices  32.1 us (28%)
  Pallas kernels  20.3 us (18%)
  local copies, waits for them, and re-layouts  8.14 us (7%)
  other arithmetic  3.33 us (3%)
  between operations  1.15 us (1%)
    ppermute x35, starting transfers between devices, send(): return lax.ppermute(x, AXES, pairs)  48.4 us
    ppermute x35, waiting for transfers between devices, send(): return lax.ppermute(x, AXES, pairs)  32.1 us
    pallas_call x6, Pallas kernels, products(): pl.pallas_call(functools.partial(product_kernel, transpose, cap, n_out, l...  20.3 us
    unnamed x8, local copies, waits for them, and re-layouts  5.04 us
  transfers between devices with their start and end apart: 35, of which 17 were waited for; matrix products, arithmetic and copies ran while one was open for 5% of the time, Pallas kernels for 18%

profile of v2, /device:TPU:5, one launch (start us, length us, event | category | flops | bytes accessed | tf_op | source)
XLA Modules:
  0.0 113.5 jit_solution(1935686302117014583)
XLA Ops:
  0.0 0.7 collective-permute-start.4
  0.7 0.9 reshape.25
  1.6 0.7 broadcast_in_dim.34
  3.2 0.7 pad_add_fusion
  3.8 0.4 collective-permute-start.3
  4.3 1.4 %collective-permute-start = (f32[4,40,128]{2,1,0:T(8,128)S(1)}, f32[4,40,128]{2,1,0:T(8,128)S(1)}, u32[]{:S(2)}, u32[]{:S(2)}) collective-permute-start(f32[4,40,128]{2,1,0:T(8,128)S(1)} %get-tuple-element.78), channel_id=1, source_target_pairs={{0,2},{1,3},{2,0},{3,1},{4,6},{5,7},{6,4},{7,5},{8,10},{9,11},{10,... | collective-permute-start | bytes 245768 | tf_op jit(solution)/shard_map/ppermute | solution.py:191
  5.7 0.8 compare_select_fusion.37
  6.5 1.1 collective-permute-done.3
  7.6 0.5 slice.106
  8.1 0.7 compare_select_fusion.35
  8.8 0.7 concatenate.50.meta_in
  9.7 2.4 %collective-permute-start.6 = (bf16[16,32,128]{2,1,0:T(8,128)(2,1)S(1)}, bf16[16,32,128]{2,1,0:T(8,128)(2,1)S(1)}, u32[]{:S(2)}, u32[]{:S(2)}) collective-permute-start(bf16[16,32,128]{2,1,0:T(8,128)(2,1)S(1)} %multiply_convert_fusion.2.vecs_in), channel_id=1, source_target_pairs={{0,16},{1,17},{2,18},{3,19},{4,20},{5,21},{6,22},{7,23},{8,24},{9,... | collective-permute-start | bytes 393224 | tf_op jit(solution)/shard_map/ppermute | solution.py:191
  12.1 2.2 %copy-done = bf16[1,1,128,128,128]{4,3,2,1,0:T(8,128)(2,1)S(1)} copy-done((bf16[1,1,128,128,128]{4,3,2,1,0:T(8,128)(2,1)S(1)}, bf16[1,1,128,128,128]{4,3,2,1,0:T(8,128)(2,1)}, u32[]{:S(2)}) %copy-start) | copy-done | bytes 4194328
  14.3 3.2 %transposed.3 = (f32[16,32,128]{2,1,0:T(8,128)S(1)}, f32[16,32,128]{2,1,0:T(8,128)S(1)}, bf16[16,32,128]{2,1,0:T(8,128)(2,1)S(1)}, bf16[16,32,128]{2,1,0:T(8,128)(2,1)S(1)}) custom-call(s32[1152]{0:T(1024)S(1)} %concatenate.50.meta_in, bf16[16,32,128]{2,1,0:T(8,128)(2,1)S(1)} %multiply_convert_fusion.2.vecs_in, bf16[128,128,128]{2,1,0:T(8,128)(2,1)S(1)} %bitcast.67, ...), custom_call_target="tpu_custom_call" | custom-call | flops 268435456 | bytes 655360 | tf_op jit(solution)/shard_map/transposed/pallas_call | solution.py:154
  17.6 0.6 collective-permute-done.6
  18.2 1.2 %collective-permute-start.7 = (bf16[16,32,128]{2,1,0:T(8,128)(2,1)S(1)}, bf16[16,32,128]{2,1,0:T(8,128)(2,1)S(1)}, u32[]{:S(2)}, u32[]{:S(2)}) collective-permute-start(bf16[16,32,128]{2,1,0:T(8,128)(2,1)S(1)} %maximum_select_fusion.1), channel_id=1, source_target_pairs={{0,8},{1,9},{2,10},{3,11},{4,12},{5,13},{6,14},{7,15},{8,0},{9,1},... | collective-permute-start | bytes 393224 | tf_op jit(solution)/shard_map/ppermute | solution.py:191
  19.5 1.3 %collective-permute-start.9 = (bf16[16,32,128]{2,1,0:T(8,128)(2,1)S(1)}, bf16[16,32,128]{2,1,0:T(8,128)(2,1)S(1)}, u32[]{:S(2)}, u32[]{:S(2)}) collective-permute-start(bf16[16,32,128]{2,1,0:T(8,128)(2,1)S(1)} %maximum_select_fusion.1), channel_id=1, source_target_pairs={{0,12},{1,13},{2,14},{3,15},{4,8},{5,9},{6,10},{7,11},{8,4},{9,5},... | collective-permute-start | bytes 393224 | tf_op jit(solution)/shard_map/ppermute | solution.py:191
  20.8 0.3 collective-permute-start.8
  21.1 1.0 collective-permute-done.7
  22.1 3.8 %collective-permute-start.10 = (bf16[16,48,128]{2,1,0:T(8,128)(2,1)S(1)}, bf16[16,48,128]{2,1,0:T(8,128)(2,1)S(1)}, u32[]{:S(2)}, u32[]{:S(2)}) collective-permute-start(bf16[16,48,128]{2,1,0:T(8,128)(2,1)S(1)} %pad_maximum_fusion.4), channel_id=1, source_target_pairs={{0,16},{1,17},{2,18},{3,19},{4,20},{5,21},{6,22},{7,23},{8,24},{9,... | collective-permute-start | bytes 589832 | tf_op jit(solution)/shard_map/ppermute | solution.py:191
  26.0 1.2 %collective-permute-start.5 = (bf16[16,32,128]{2,1,0:T(8,128)(2,1)S(1)}, bf16[16,32,128]{2,1,0:T(8,128)(2,1)S(1)}, u32[]{:S(2)}, u32[]{:S(2)}) collective-permute-start(bf16[16,32,128]{2,1,0:T(8,128)(2,1)S(1)} %get-tuple-element.42.refs_3_), channel_id=1, source_target_pairs={{0,4},{1,5},{2,6},{3,7},{4,0},{5,1},{6,2},{7,3},{8,12},{9,13},{10,... | collective-permute-start | bytes 393224 | tf_op jit(solution)/shard_map/ppermute | solution.py:191
  27.2 0.3 collective-permute-start.11
  27.4 0.4 collective-permute-done.8
  27.9 2.2 %copy-done.1 = bf16[1,1,128,128,128]{4,3,2,1,0:T(8,128)(2,1)S(1)} copy-done((bf16[1,1,128,128,128]{4,3,2,1,0:T(8,128)(2,1)S(1)}, bf16[1,1,128,128,128]{4,3,2,1,0:T(8,128)(2,1)}, u32[]{:S(2)}) %copy-start.1) | copy-done | bytes 4194328
  30.1 3.5 %direct.3 = bf16[16,32,128]{2,1,0:T(8,128)(2,1)S(1)} custom-call(s32[1152]{0:T(1024)S(1)} %concatenate.50.meta_in, bf16[64,32,128]{2,1,0:T(8,128)(2,1)S(1)} %pad_maximum_fusion.vecs_in, bf16[128,128,128]{2,1,0:T(8,128)(2,1)S(1)} %bitcast.68, bf16[128,128,128]{2,1,0:T(8,128)(2,1)} %collective-permute-done.4.refs_1_, ...), custom_call_target="tpu_custom_call" | custom-call | flops 268435456 | bytes 655360 | tf_op jit(solution)/shard_map/direct/pallas_call | solution.py:154
  33.7 0.3 collective-permute-done.10
  34.1 2.0 %collective-permute-start.12 = (bf16[16,32,128]{2,1,0:T(8,128)(2,1)S(1)}, bf16[16,32,128]{2,1,0:T(8,128)(2,1)S(1)}, u32[]{:S(2)}, u32[]{:S(2)}) collective-permute-start(bf16[16,32,128]{2,1,0:T(8,128)(2,1)S(1)} %add_convert_fusion.2), channel_id=1, source_target_pairs={{0,8},{1,9},{2,10},{3,11},{4,12},{5,13},{6,14},{7,15},{8,0},{9,1},... | collective-permute-start | bytes 393224 | tf_op jit(solution)/shard_map/ppermute | solution.py:191
  36.1 0.2 collective-permute-start.13
  36.3 2.1 %collective-permute-done.12 = bf16[16,32,128]{2,1,0:T(8,128)(2,1)S(1)} collective-permute-done((bf16[16,32,128]{2,1,0:T(8,128)(2,1)S(1)}, bf16[16,32,128]{2,1,0:T(8,128)(2,1)S(1)}, u32[]{:S(2)}, u32[]{:S(2)}) %collective-permute-start.12) | collective-permute-done | bytes 131104 | tf_op jit(solution)/shard_map/ppermute | solution.py:191
  38.5 1.8 %collective-permute-done.13 = bf16[16,32,128]{2,1,0:T(8,128)(2,1)S(1)} collective-permute-done((bf16[16,32,128]{2,1,0:T(8,128)(2,1)S(1)}, bf16[16,32,128]{2,1,0:T(8,128)(2,1)S(1)}, u32[]{:S(2)}, u32[]{:S(2)}) %collective-permute-start.13) | collective-permute-done | bytes 131104 | tf_op jit(solution)/shard_map/ppermute | solution.py:191
  40.2 0.1 fusion.34
  40.3 3.2 %collective-permute-start.14 = (bf16[16,32,128]{2,1,0:T(8,128)(2,1)S(1)}, bf16[16,32,128]{2,1,0:T(8,128)(2,1)S(1)}, u32[]{:S(2)}, u32[]{:S(2)}) collective-permute-start(bf16[16,32,128]{2,1,0:T(8,128)(2,1)S(1)} %get-tuple-element.63), channel_id=1, source_target_pairs={{0,16},{1,17},{2,18},{3,19},{4,20},{5,21},{6,22},{7,23},{8,24},{9,... | collective-permute-start | bytes 393224 | tf_op jit(solution)/shard_map/ppermute | solution.py:191
  43.5 3.3 %collective-permute-done.14 = bf16[16,32,128]{2,1,0:T(8,128)(2,1)S(1)} collective-permute-done((bf16[16,32,128]{2,1,0:T(8,128)(2,1)S(1)}, bf16[16,32,128]{2,1,0:T(8,128)(2,1)S(1)}, u32[]{:S(2)}, u32[]{:S(2)}) %collective-permute-start.14) | collective-permute-done | bytes 131104 | tf_op jit(solution)/shard_map/ppermute | solution.py:191
  46.8 0.1 multiply_convert_fusion.1
  46.9 0.2 collective-permute-start.15
  47.1 1.8 %collective-permute-start.21 = (bf16[16,32,128]{2,1,0:T(8,128)(2,1)S(1)}, bf16[16,32,128]{2,1,0:T(8,128)(2,1)S(1)}, u32[]{:S(2)}, u32[]{:S(2)}) collective-permute-start(bf16[16,32,128]{2,1,0:T(8,128)(2,1)S(1)} %get-tuple-element.61), channel_id=1, source_target_pairs={{0,12},{1,13},{2,14},{3,15},{4,8},{5,9},{6,10},{7,11},{8,4},{9,5},... | collective-permute-start | bytes 393224 | tf_op jit(solution)/shard_map/ppermute | solution.py:191
  48.9 2.6 %collective-permute-start.20 = (bf16[16,32,128]{2,1,0:T(8,128)(2,1)S(1)}, bf16[16,32,128]{2,1,0:T(8,128)(2,1)S(1)}, u32[]{:S(2)}, u32[]{:S(2)}) collective-permute-start(bf16[16,32,128]{2,1,0:T(8,128)(2,1)S(1)} %get-tuple-element.61), channel_id=1, source_target_pairs={{0,4},{1,5},{2,6},{3,7},{4,0},{5,1},{6,2},{7,3},{8,12},{9,13},{10,... | collective-permute-start | bytes 393224 | tf_op jit(solution)/shard_map/ppermute | solution.py:191
  51.5 1.2 %collective-permute-start.19 = (bf16[16,32,128]{2,1,0:T(8,128)(2,1)S(1)}, bf16[16,32,128]{2,1,0:T(8,128)(2,1)S(1)}, u32[]{:S(2)}, u32[]{:S(2)}) collective-permute-start(bf16[16,32,128]{2,1,0:T(8,128)(2,1)S(1)} %get-tuple-element.61), channel_id=1, source_target_pairs={{0,8},{1,9},{2,10},{3,11},{4,12},{5,13},{6,14},{7,15},{8,0},{9,1},... | collective-permute-start | bytes 393224 | tf_op jit(solution)/shard_map/ppermute | solution.py:191
  52.7 3.2 %transposed.4 = (f32[16,32,128]{2,1,0:T(8,128)S(1)}, f32[16,32,128]{2,1,0:T(8,128)S(1)}, bf16[16,32,128]{2,1,0:T(8,128)(2,1)S(1)}, bf16[16,32,128]{2,1,0:T(8,128)(2,1)S(1)}) custom-call(s32[1152]{0:T(1024)S(1)} %concatenate.50.meta_in, bf16[16,32,128]{2,1,0:T(8,128)(2,1)S(1)} %broadcast_select_fusion.1.vecs_in, bf16[128,128,128]{2,1,0:T(8,128)(2,1)S(1)} %bitcast.69, ...), custom_call_target="tpu_custom_call" | custom-call | flops 268435456 | bytes 655360 | tf_op jit(solution)/shard_map/transposed/pallas_call | solution.py:154
  55.9 1.5 %collective-permute-start.16 = (bf16[16,32,128]{2,1,0:T(8,128)(2,1)S(1)}, bf16[16,32,128]{2,1,0:T(8,128)(2,1)S(1)}, u32[]{:S(2)}, u32[]{:S(2)}) collective-permute-start(bf16[16,32,128]{2,1,0:T(8,128)(2,1)S(1)} %get-tuple-element.50.refs_2_), channel_id=1, source_target_pairs={{0,4},{1,5},{2,6},{3,7},{4,0},{5,1},{6,2},{7,3},{8,12},{9,13},{10,... | collective-permute-start | bytes 393224 | tf_op jit(solution)/shard_map/ppermute | solution.py:191
  57.5 0.4 collective-permute-done.19
  57.9 3.5 %direct.4 = bf16[16,32,128]{2,1,0:T(8,128)(2,1)S(1)} custom-call(s32[1152]{0:T(1024)S(1)} %concatenate.50.meta_in, bf16[64,32,128]{2,1,0:T(8,128)(2,1)S(1)} %pad_maximum_fusion.1.vecs_in, bf16[128,128,128]{2,1,0:T(8,128)(2,1)S(1)} %bitcast.70, bf16[128,128,128]{2,1,0:T(8,128)(2,1)} %collective-permute-done.4.refs_1_, ...), custom_call_target="tpu_custom_call" | custom-call | flops 268435456 | bytes 655360 | tf_op jit(solution)/shard_map/direct/pallas_call | solution.py:154
  61.6 1.8 %collective-permute-start.18 = (bf16[16,32,128]{2,1,0:T(8,128)(2,1)S(1)}, bf16[16,32,128]{2,1,0:T(8,128)(2,1)S(1)}, u32[]{:S(2)}, u32[]{:S(2)}) collective-permute-start(bf16[16,32,128]{2,1,0:T(8,128)(2,1)S(1)} %add_convert_fusion.1), channel_id=1, source_target_pairs={{0,8},{1,9},{2,10},{3,11},{4,12},{5,13},{6,14},{7,15},{8,0},{9,1},... | collective-permute-start | bytes 393224 | tf_op jit(solution)/shard_map/ppermute | solution.py:191
  63.3 2.0 %collective-permute-done.22 = bf16[16,32,128]{2,1,0:T(8,128)(2,1)S(1)} collective-permute-done((bf16[16,32,128]{2,1,0:T(8,128)(2,1)S(1)}, bf16[16,32,128]{2,1,0:T(8,128)(2,1)S(1)}, u32[]{:S(2)}, u32[]{:S(2)}) %collective-permute-start.22) | collective-permute-done | bytes 131104 | tf_op jit(solution)/shard_map/ppermute | solution.py:191
  65.3 0.4 collective-permute-done.18
  65.7 0.1 fusion.33
  65.8 1.6 %collective-permute-start.23 = (bf16[16,32,128]{2,1,0:T(8,128)(2,1)S(1)}, bf16[16,32,128]{2,1,0:T(8,128)(2,1)S(1)}, u32[]{:S(2)}, u32[]{:S(2)}) collective-permute-start(bf16[16,32,128]{2,1,0:T(8,128)(2,1)S(1)} %get-tuple-element.59), channel_id=1, source_target_pairs={{0,16},{1,17},{2,18},{3,19},{4,20},{5,21},{6,22},{7,23},{8,24},{9,... | collective-permute-start | bytes 393224 | tf_op jit(solution)/shard_map/ppermute | solution.py:191
  67.4 3.3 %collective-permute-done.23 = bf16[16,32,128]{2,1,0:T(8,128)(2,1)S(1)} collective-permute-done((bf16[16,32,128]{2,1,0:T(8,128)(2,1)S(1)}, bf16[16,32,128]{2,1,0:T(8,128)(2,1)S(1)}, u32[]{:S(2)}, u32[]{:S(2)}) %collective-permute-start.23) | collective-permute-done | bytes 131104 | tf_op jit(solution)/shard_map/ppermute | solution.py:191
  70.7 0.1 multiply_convert_fusion
  70.8 3.4 %collective-permute-start.24 = (bf16[16,32,128]{2,1,0:T(8,128)(2,1)S(1)}, bf16[16,32,128]{2,1,0:T(8,128)(2,1)S(1)}, u32[]{:S(2)}, u32[]{:S(2)}) collective-permute-start(bf16[16,32,128]{2,1,0:T(8,128)(2,1)S(1)} %get-tuple-element.57), channel_id=1, source_target_pairs={{0,2},{1,3},{2,0},{3,1},{4,6},{5,7},{6,4},{7,5},{8,10},{9,11},{10,... | collective-permute-start | bytes 393224 | tf_op jit(solution)/shard_map/ppermute | solution.py:191
  74.2 0.8 collective-permute-start.29
  75.1 1.8 %collective-permute-start.28 = (bf16[16,32,128]{2,1,0:T(8,128)(2,1)S(1)}, bf16[16,32,128]{2,1,0:T(8,128)(2,1)S(1)}, u32[]{:S(2)}, u32[]{:S(2)}) collective-permute-start(bf16[16,32,128]{2,1,0:T(8,128)(2,1)S(1)} %get-tuple-element.57), channel_id=1, source_target_pairs={{0,8},{1,9},{2,10},{3,11},{4,12},{5,13},{6,14},{7,15},{8,0},{9,1},... | collective-permute-start | bytes 393224 | tf_op jit(solution)/shard_map/ppermute | solution.py:191
  76.9 3.2 %transposed.5 = (f32[16,32,128]{2,1,0:T(8,128)S(1)}, f32[16,32,128]{2,1,0:T(8,128)S(1)}, bf16[16,32,128]{2,1,0:T(8,128)(2,1)S(1)}, bf16[16,32,128]{2,1,0:T(8,128)(2,1)S(1)}) custom-call(s32[1152]{0:T(1024)S(1)} %concatenate.50.meta_in, bf16[16,32,128]{2,1,0:T(8,128)(2,1)S(1)} %broadcast_select_fusion.vecs_in, bf16[128,128,128]{2,1,0:T(8,128)(2,1)S(1)} %bitcast.71, ...), custom_call_target="tpu_custom_call" | custom-call | flops 268435456 | bytes 655360 | tf_op jit(solution)/shard_map/transposed/pallas_call | solution.py:154
  80.2 1.5 %collective-permute-start.26 = (bf16[16,32,128]{2,1,0:T(8,128)(2,1)S(1)}, bf16[16,32,128]{2,1,0:T(8,128)(2,1)S(1)}, u32[]{:S(2)}, u32[]{:S(2)}) collective-permute-start(bf16[16,32,128]{2,1,0:T(8,128)(2,1)S(1)} %get-tuple-element.56.refs_3_), channel_id=1, source_target_pairs={{0,4},{1,5},{2,6},{3,7},{4,0},{5,1},{6,2},{7,3},{8,12},{9,13},{10,... | collective-permute-start | bytes 393224 | tf_op jit(solution)/shard_map/ppermute | solution.py:191
  81.8 3.5 %direct.5 = bf16[16,32,128]{2,1,0:T(8,128)(2,1)S(1)} custom-call(s32[1152]{0:T(1024)S(1)} %concatenate.50.meta_in, bf16[64,32,128]{2,1,0:T(8,128)(2,1)S(1)} %pad_maximum_fusion.2.vecs_in, bf16[128,128,128]{2,1,0:T(8,128)(2,1)S(1)} %bitcast.72, bf16[128,128,128]{2,1,0:T(8,128)(2,1)} %collective-permute-done.4.refs_1_, ...), custom_call_target="tpu_custom_call" | custom-call | flops 268435456 | bytes 655360 | tf_op jit(solution)/shard_map/direct/pallas_call | solution.py:154
  85.4 2.6 %collective-permute-done.26 = bf16[16,32,128]{2,1,0:T(8,128)(2,1)S(1)} collective-permute-done((bf16[16,32,128]{2,1,0:T(8,128)(2,1)S(1)}, bf16[16,32,128]{2,1,0:T(8,128)(2,1)S(1)}, u32[]{:S(2)}, u32[]{:S(2)}) %collective-permute-start.26) | collective-permute-done | bytes 131104 | tf_op jit(solution)/shard_map/ppermute | solution.py:191
  88.1 1.1 collective-permute-done.31
  89.2 3.0 %collective-permute-done.27 = bf16[16,32,128]{2,1,0:T(8,128)(2,1)S(1)} collective-permute-done((bf16[16,32,128]{2,1,0:T(8,128)(2,1)S(1)}, bf16[16,32,128]{2,1,0:T(8,128)(2,1)S(1)}, u32[]{:S(2)}, u32[]{:S(2)}) %collective-permute-start.27) | collective-permute-done | bytes 131104 | tf_op jit(solution)/shard_map/ppermute | solution.py:191
  92.3 1.0 collective-permute-start.32
  93.3 3.6 %collective-permute-done.32 = bf16[8,32,128]{2,1,0:T(8,128)(2,1)S(1)} collective-permute-done((bf16[8,32,128]{2,1,0:T(8,128)(2,1)S(1)}, bf16[8,32,128]{2,1,0:T(8,128)(2,1)S(1)}, u32[]{:S(2)}, u32[]{:S(2)}) %collective-permute-start.32) | collective-permute-done | bytes 65568 | tf_op jit(solution)/shard_map/ppermute | solution.py:191
  97.0 7.6 %collective-permute-start.34 = (f32[4,32,128]{2,1,0:T(8,128)S(1)}, f32[4,32,128]{2,1,0:T(8,128)S(1)}, u32[]{:S(2)}, u32[]{:S(2)}) collective-permute-start(f32[4,32,128]{2,1,0:T(8,128)S(1)} %get-tuple-element.81), channel_id=1, source_target_pairs={{1,0},{0,1},{17,2},{16,3},{5,4},{4,5},{21,6},{20,7},{9,8},{8,9},{2... | collective-permute-start | bytes 196616 | tf_op jit(solution)/shard_map/ppermute | solution.py:191
  104.7 2.8 %collective-permute-start.33 = (f32[4,32,128]{2,1,0:T(8,128)S(1)}, f32[4,32,128]{2,1,0:T(8,128)S(1)}, u32[]{:S(2)}, u32[]{:S(2)}) collective-permute-start(f32[4,32,128]{2,1,0:T(8,128)S(1)} %get-tuple-element.82), channel_id=1, source_target_pairs={{0,0},{1,1},{16,2},{17,3},{4,4},{5,5},{20,6},{21,7},{8,8},{9,9},{2... | collective-permute-start | bytes 196616 | tf_op jit(solution)/shard_map/ppermute | solution.py:191
  107.4 5.2 %collective-permute-done.33 = f32[4,32,128]{2,1,0:T(8,128)S(1)} collective-permute-done((f32[4,32,128]{2,1,0:T(8,128)S(1)}, f32[4,32,128]{2,1,0:T(8,128)S(1)}, u32[]{:S(2)}, u32[]{:S(2)}) %collective-permute-start.33) | collective-permute-done | bytes 65568 | tf_op jit(solution)/shard_map/ppermute | solution.py:191
  112.8 0.7 copy.15
  (72 shorter events, 1.6 us)
Async XLA Ops:
  0.0 9.6 %collective-permute-start.4 = (bf16[128,128,128]{2,1,0:T(8,128)(2,1)}, bf16[128,128,128]{2,1,0:T(8,128)(2,1)}, u32[]{:S(2)}, u32[]{:S(2)}) collective-permute-start(bf16[128,128,128]{2,1,0:T(8,128)(2,1)} %bitcast.66), channel_id=1, source_target_pairs={{0,1},{1,0},{2,3},{3,2},{4,5},{5,4},{6,7},{7,6},{8,9},{9,8},{10,11... | collective-permute-start | bytes 12582920 | tf_op jit(solution)/shard_map/ppermute | solution.py:191
  2.4 7.2 %collective-permute-start.2 = (f32[4,40,128]{2,1,0:T(8,128)S(1)}, f32[4,40,128]{2,1,0:T(8,128)S(1)}, u32[]{:S(2)}, u32[]{:S(2)}) collective-permute-start(f32[4,40,128]{2,1,0:T(8,128)S(1)} %get-tuple-element.77), channel_id=1, source_target_pairs={{0,1},{1,0},{2,3},{3,2},{4,5},{5,4},{6,7},{7,6},{8,9},{9,8},{10,11... | collective-permute-start | bytes 245768 | tf_op jit(solution)/shard_map/ppermute | solution.py:191
  2.4 7.1 %collective-permute-start.1 = (f32[4,40,128]{2,1,0:T(8,128)S(1)}, f32[4,40,128]{2,1,0:T(8,128)S(1)}, u32[]{:S(2)}, u32[]{:S(2)}) collective-permute-start(f32[4,40,128]{2,1,0:T(8,128)S(1)} %get-tuple-element.77), channel_id=1, source_target_pairs={{0,3},{1,2},{2,1},{3,0},{4,7},{5,6},{6,5},{7,4},{8,11},{9,10},{10,... | collective-permute-start | bytes 245768 | tf_op jit(solution)/shard_map/ppermute | solution.py:191
  3.8 3.7 %collective-permute-start.3 = (s32[257]{0:T(512)S(1)}, s32[257]{0:T(512)S(1)}, u32[]{:S(2)}, u32[]{:S(2)}) collective-permute-start(s32[257]{0:T(512)S(1)} %pad_add_fusion), channel_id=1, source_target_pairs={{0,1},{1,0},{2,3},{3,2},{4,5},{5,4},{6,7},{7,6},{8,9},{9,8},{10,11... | collective-permute-start | bytes 3092 | tf_op jit(solution)/shard_map/ppermute | solution.py:191
  4.3 5.3 %collective-permute-start = (f32[4,40,128]{2,1,0:T(8,128)S(1)}, f32[4,40,128]{2,1,0:T(8,128)S(1)}, u32[]{:S(2)}, u32[]{:S(2)}) collective-permute-start(f32[4,40,128]{2,1,0:T(8,128)S(1)} %get-tuple-element.78), channel_id=1, source_target_pairs={{0,2},{1,3},{2,0},{3,1},{4,6},{5,7},{6,4},{7,5},{8,10},{9,11},{10,... | collective-permute-start | bytes 245768 | tf_op jit(solution)/shard_map/ppermute | solution.py:191
  9.7 8.5 %collective-permute-start.6 = (bf16[16,32,128]{2,1,0:T(8,128)(2,1)S(1)}, bf16[16,32,128]{2,1,0:T(8,128)(2,1)S(1)}, u32[]{:S(2)}, u32[]{:S(2)}) collective-permute-start(bf16[16,32,128]{2,1,0:T(8,128)(2,1)S(1)} %multiply_convert_fusion.2.vecs_in), channel_id=1, source_target_pairs={{0,16},{1,17},{2,18},{3,19},{4,20},{5,21},{6,22},{7,23},{8,24},{9,... | collective-permute-start | bytes 393224 | tf_op jit(solution)/shard_map/ppermute | solution.py:191
  12.1 2.2 %copy-start = (bf16[1,1,128,128,128]{4,3,2,1,0:T(8,128)(2,1)S(1)}, bf16[1,1,128,128,128]{4,3,2,1,0:T(8,128)(2,1)}, u32[]{:S(2)}) copy-start(bf16[1,1,128,128,128]{4,3,2,1,0:T(8,128)(2,1)} %param.7) | copy-start | bytes 12582916
  18.2 3.9 %collective-permute-start.7 = (bf16[16,32,128]{2,1,0:T(8,128)(2,1)S(1)}, bf16[16,32,128]{2,1,0:T(8,128)(2,1)S(1)}, u32[]{:S(2)}, u32[]{:S(2)}) collective-permute-start(bf16[16,32,128]{2,1,0:T(8,128)(2,1)S(1)} %maximum_select_fusion.1), channel_id=1, source_target_pairs={{0,8},{1,9},{2,10},{3,11},{4,12},{5,13},{6,14},{7,15},{8,0},{9,1},... | collective-permute-start | bytes 393224 | tf_op jit(solution)/shard_map/ppermute | solution.py:191
  19.5 8.0 %collective-permute-start.9 = (bf16[16,32,128]{2,1,0:T(8,128)(2,1)S(1)}, bf16[16,32,128]{2,1,0:T(8,128)(2,1)S(1)}, u32[]{:S(2)}, u32[]{:S(2)}) collective-permute-start(bf16[16,32,128]{2,1,0:T(8,128)(2,1)S(1)} %maximum_select_fusion.1), channel_id=1, source_target_pairs={{0,12},{1,13},{2,14},{3,15},{4,8},{5,9},{6,10},{7,11},{8,4},{9,5},... | collective-permute-start | bytes 393224 | tf_op jit(solution)/shard_map/ppermute | solution.py:191
  20.8 7.0 %collective-permute-start.8 = (bf16[16,32,128]{2,1,0:T(8,128)(2,1)S(1)}, bf16[16,32,128]{2,1,0:T(8,128)(2,1)S(1)}, u32[]{:S(2)}, u32[]{:S(2)}) collective-permute-start(bf16[16,32,128]{2,1,0:T(8,128)(2,1)S(1)} %maximum_select_fusion.1), channel_id=1, source_target_pairs={{0,4},{1,5},{2,6},{3,7},{4,0},{5,1},{6,2},{7,3},{8,12},{9,13},{10,... | collective-permute-start | bytes 393224 | tf_op jit(solution)/shard_map/ppermute | solution.py:191
  22.1 11.8 %collective-permute-start.10 = (bf16[16,48,128]{2,1,0:T(8,128)(2,1)S(1)}, bf16[16,48,128]{2,1,0:T(8,128)(2,1)S(1)}, u32[]{:S(2)}, u32[]{:S(2)}) collective-permute-start(bf16[16,48,128]{2,1,0:T(8,128)(2,1)S(1)} %pad_maximum_fusion.4), channel_id=1, source_target_pairs={{0,16},{1,17},{2,18},{3,19},{4,20},{5,21},{6,22},{7,23},{8,24},{9,... | collective-permute-start | bytes 589832 | tf_op jit(solution)/shard_map/ppermute | solution.py:191
  26.0 7.7 %collective-permute-start.5 = (bf16[16,32,128]{2,1,0:T(8,128)(2,1)S(1)}, bf16[16,32,128]{2,1,0:T(8,128)(2,1)S(1)}, u32[]{:S(2)}, u32[]{:S(2)}) collective-permute-start(bf16[16,32,128]{2,1,0:T(8,128)(2,1)S(1)} %get-tuple-element.42.refs_3_), channel_id=1, source_target_pairs={{0,4},{1,5},{2,6},{3,7},{4,0},{5,1},{6,2},{7,3},{8,12},{9,13},{10,... | collective-permute-start | bytes 393224 | tf_op jit(solution)/shard_map/ppermute | solution.py:191
  27.2 9.1 %collective-permute-start.11 = (bf16[16,32,128]{2,1,0:T(8,128)(2,1)S(1)}, bf16[16,32,128]{2,1,0:T(8,128)(2,1)S(1)}, u32[]{:S(2)}, u32[]{:S(2)}) collective-permute-start(bf16[16,32,128]{2,1,0:T(8,128)(2,1)S(1)} %get-tuple-element.41.refs_2_), channel_id=1, source_target_pairs={{0,4},{1,5},{2,6},{3,7},{4,0},{5,1},{6,2},{7,3},{8,12},{9,13},{10,... | collective-permute-start | bytes 393224 | tf_op jit(solution)/shard_map/ppermute | solution.py:191
  27.9 2.2 %copy-start.1 = (bf16[1,1,128,128,128]{4,3,2,1,0:T(8,128)(2,1)S(1)}, bf16[1,1,128,128,128]{4,3,2,1,0:T(8,128)(2,1)}, u32[]{:S(2)}) copy-start(bf16[1,1,128,128,128]{4,3,2,1,0:T(8,128)(2,1)} %param.7) | copy-start | bytes 12582916
  34.1 4.4 %collective-permute-start.12 = (bf16[16,32,128]{2,1,0:T(8,128)(2,1)S(1)}, bf16[16,32,128]{2,1,0:T(8,128)(2,1)S(1)}, u32[]{:S(2)}, u32[]{:S(2)}) collective-permute-start(bf16[16,32,128]{2,1,0:T(8,128)(2,1)S(1)} %add_convert_fusion.2), channel_id=1, source_target_pairs={{0,8},{1,9},{2,10},{3,11},{4,12},{5,13},{6,14},{7,15},{8,0},{9,1},... | collective-permute-start | bytes 393224 | tf_op jit(solution)/shard_map/ppermute | solution.py:191
  36.1 4.1 %collective-permute-start.13 = (bf16[16,32,128]{2,1,0:T(8,128)(2,1)S(1)}, bf16[16,32,128]{2,1,0:T(8,128)(2,1)S(1)}, u32[]{:S(2)}, u32[]{:S(2)}) collective-permute-start(bf16[16,32,128]{2,1,0:T(8,128)(2,1)S(1)} %direct.3), channel_id=1, source_target_pairs={{0,2},{1,3},{2,0},{3,1},{4,6},{5,7},{6,4},{7,5},{8,10},{9,11},{10,... | collective-permute-start | bytes 393224 | tf_op jit(solution)/shard_map/ppermute | solution.py:191
  40.3 6.4 %collective-permute-start.14 = (bf16[16,32,128]{2,1,0:T(8,128)(2,1)S(1)}, bf16[16,32,128]{2,1,0:T(8,128)(2,1)S(1)}, u32[]{:S(2)}, u32[]{:S(2)}) collective-permute-start(bf16[16,32,128]{2,1,0:T(8,128)(2,1)S(1)} %get-tuple-element.63), channel_id=1, source_target_pairs={{0,16},{1,17},{2,18},{3,19},{4,20},{5,21},{6,22},{7,23},{8,24},{9,... | collective-permute-start | bytes 393224 | tf_op jit(solution)/shard_map/ppermute | solution.py:191
  46.9 5.8 %collective-permute-start.15 = (bf16[16,32,128]{2,1,0:T(8,128)(2,1)S(1)}, bf16[16,32,128]{2,1,0:T(8,128)(2,1)S(1)}, u32[]{:S(2)}, u32[]{:S(2)}) collective-permute-start(bf16[16,32,128]{2,1,0:T(8,128)(2,1)S(1)} %get-tuple-element.61), channel_id=1, source_target_pairs={{0,2},{1,3},{2,0},{3,1},{4,6},{5,7},{6,4},{7,5},{8,10},{9,11},{10,... | collective-permute-start | bytes 393224 | tf_op jit(solution)/shard_map/ppermute | solution.py:191
  47.1 10.3 %collective-permute-start.21 = (bf16[16,32,128]{2,1,0:T(8,128)(2,1)S(1)}, bf16[16,32,128]{2,1,0:T(8,128)(2,1)S(1)}, u32[]{:S(2)}, u32[]{:S(2)}) collective-permute-start(bf16[16,32,128]{2,1,0:T(8,128)(2,1)S(1)} %get-tuple-element.61), channel_id=1, source_target_pairs={{0,12},{1,13},{2,14},{3,15},{4,8},{5,9},{6,10},{7,11},{8,4},{9,5},... | collective-permute-start | bytes 393224 | tf_op jit(solution)/shard_map/ppermute | solution.py:191
  48.9 8.6 %collective-permute-start.20 = (bf16[16,32,128]{2,1,0:T(8,128)(2,1)S(1)}, bf16[16,32,128]{2,1,0:T(8,128)(2,1)S(1)}, u32[]{:S(2)}, u32[]{:S(2)}) collective-permute-start(bf16[16,32,128]{2,1,0:T(8,128)(2,1)S(1)} %get-tuple-element.61), channel_id=1, source_target_pairs={{0,4},{1,5},{2,6},{3,7},{4,0},{5,1},{6,2},{7,3},{8,12},{9,13},{10,... | collective-permute-start | bytes 393224 | tf_op jit(solution)/shard_map/ppermute | solution.py:191
  51.5 6.4 %collective-permute-start.19 = (bf16[16,32,128]{2,1,0:T(8,128)(2,1)S(1)}, bf16[16,32,128]{2,1,0:T(8,128)(2,1)S(1)}, u32[]{:S(2)}, u32[]{:S(2)}) collective-permute-start(bf16[16,32,128]{2,1,0:T(8,128)(2,1)S(1)} %get-tuple-element.61), channel_id=1, source_target_pairs={{0,8},{1,9},{2,10},{3,11},{4,12},{5,13},{6,14},{7,15},{8,0},{9,1},... | collective-permute-start | bytes 393224 | tf_op jit(solution)/shard_map/ppermute | solution.py:191
  55.9 9.4 %collective-permute-start.16 = (bf16[16,32,128]{2,1,0:T(8,128)(2,1)S(1)}, bf16[16,32,128]{2,1,0:T(8,128)(2,1)S(1)}, u32[]{:S(2)}, u32[]{:S(2)}) collective-permute-start(bf16[16,32,128]{2,1,0:T(8,128)(2,1)S(1)} %get-tuple-element.50.refs_2_), channel_id=1, source_target_pairs={{0,4},{1,5},{2,6},{3,7},{4,0},{5,1},{6,2},{7,3},{8,12},{9,13},{10,... | collective-permute-start | bytes 393224 | tf_op jit(solution)/shard_map/ppermute | solution.py:191
  57.4 4.2 %collective-permute-start.17 = (bf16[16,32,128]{2,1,0:T(8,128)(2,1)S(1)}, bf16[16,32,128]{2,1,0:T(8,128)(2,1)S(1)}, u32[]{:S(2)}, u32[]{:S(2)}) collective-permute-start(bf16[16,32,128]{2,1,0:T(8,128)(2,1)S(1)} %get-tuple-element.52.refs_3_), channel_id=1, source_target_pairs={{0,4},{1,5},{2,6},{3,7},{4,0},{5,1},{6,2},{7,3},{8,12},{9,13},{10,... | collective-permute-start | bytes 393224 | tf_op jit(solution)/shard_map/ppermute | solution.py:191
  61.4 3.9 %collective-permute-start.22 = (bf16[16,32,128]{2,1,0:T(8,128)(2,1)S(1)}, bf16[16,32,128]{2,1,0:T(8,128)(2,1)S(1)}, u32[]{:S(2)}, u32[]{:S(2)}) collective-permute-start(bf16[16,32,128]{2,1,0:T(8,128)(2,1)S(1)} %direct.4), channel_id=1, source_target_pairs={{0,2},{1,3},{2,0},{3,1},{4,6},{5,7},{6,4},{7,5},{8,10},{9,11},{10,... | collective-permute-start | bytes 393224 | tf_op jit(solution)/shard_map/ppermute | solution.py:191
  61.6 4.1 %collective-permute-start.18 = (bf16[16,32,128]{2,1,0:T(8,128)(2,1)S(1)}, bf16[16,32,128]{2,1,0:T(8,128)(2,1)S(1)}, u32[]{:S(2)}, u32[]{:S(2)}) collective-permute-start(bf16[16,32,128]{2,1,0:T(8,128)(2,1)S(1)} %add_convert_fusion.1), channel_id=1, source_target_pairs={{0,8},{1,9},{2,10},{3,11},{4,12},{5,13},{6,14},{7,15},{8,0},{9,1},... | collective-permute-start | bytes 393224 | tf_op jit(solution)/shard_map/ppermute | solution.py:191
  65.8 4.9 %collective-permute-start.23 = (bf16[16,32,128]{2,1,0:T(8,128)(2,1)S(1)}, bf16[16,32,128]{2,1,0:T(8,128)(2,1)S(1)}, u32[]{:S(2)}, u32[]{:S(2)}) collective-permute-start(bf16[16,32,128]{2,1,0:T(8,128)(2,1)S(1)} %get-tuple-element.59), channel_id=1, source_target_pairs={{0,16},{1,17},{2,18},{3,19},{4,20},{5,21},{6,22},{7,23},{8,24},{9,... | collective-permute-start | bytes 393224 | tf_op jit(solution)/shard_map/ppermute | solution.py:191
  70.8 6.0 %collective-permute-start.24 = (bf16[16,32,128]{2,1,0:T(8,128)(2,1)S(1)}, bf16[16,32,128]{2,1,0:T(8,128)(2,1)S(1)}, u32[]{:S(2)}, u32[]{:S(2)}) collective-permute-start(bf16[16,32,128]{2,1,0:T(8,128)(2,1)S(1)} %get-tuple-element.57), channel_id=1, source_target_pairs={{0,2},{1,3},{2,0},{3,1},{4,6},{5,7},{6,4},{7,5},{8,10},{9,11},{10,... | collective-permute-start | bytes 393224 | tf_op jit(solution)/shard_map/ppermute | solution.py:191
  74.2 7.5 %collective-permute-start.30 = (bf16[16,32,128]{2,1,0:T(8,128)(2,1)S(1)}, bf16[16,32,128]{2,1,0:T(8,128)(2,1)S(1)}, u32[]{:S(2)}, u32[]{:S(2)}) collective-permute-start(bf16[16,32,128]{2,1,0:T(8,128)(2,1)S(1)} %get-tuple-element.57), channel_id=1, source_target_pairs={{0,12},{1,13},{2,14},{3,15},{4,8},{5,9},{6,10},{7,11},{8,4},{9,5},... | collective-permute-start | bytes 393224 | tf_op jit(solution)/shard_map/ppermute | solution.py:191
  74.2 7.5 %collective-permute-start.29 = (bf16[16,32,128]{2,1,0:T(8,128)(2,1)S(1)}, bf16[16,32,128]{2,1,0:T(8,128)(2,1)S(1)}, u32[]{:S(2)}, u32[]{:S(2)}) collective-permute-start(bf16[16,32,128]{2,1,0:T(8,128)(2,1)S(1)} %get-tuple-element.57), channel_id=1, source_target_pairs={{0,4},{1,5},{2,6},{3,7},{4,0},{5,1},{6,2},{7,3},{8,12},{9,13},{10,... | collective-permute-start | bytes 393224 | tf_op jit(solution)/shard_map/ppermute | solution.py:191
  75.1 6.6 %collective-permute-start.28 = (bf16[16,32,128]{2,1,0:T(8,128)(2,1)S(1)}, bf16[16,32,128]{2,1,0:T(8,128)(2,1)S(1)}, u32[]{:S(2)}, u32[]{:S(2)}) collective-permute-start(bf16[16,32,128]{2,1,0:T(8,128)(2,1)S(1)} %get-tuple-element.57), channel_id=1, source_target_pairs={{0,8},{1,9},{2,10},{3,11},{4,12},{5,13},{6,14},{7,15},{8,0},{9,1},... | collective-permute-start | bytes 393224 | tf_op jit(solution)/shard_map/ppermute | solution.py:191
  80.1 9.1 %collective-permute-start.25 = (bf16[16,32,128]{2,1,0:T(8,128)(2,1)S(1)}, bf16[16,32,128]{2,1,0:T(8,128)(2,1)S(1)}, u32[]{:S(2)}, u32[]{:S(2)}) collective-permute-start(bf16[16,32,128]{2,1,0:T(8,128)(2,1)S(1)} %get-tuple-element.54.refs_2_), channel_id=1, source_target_pairs={{0,4},{1,5},{2,6},{3,7},{4,0},{5,1},{6,2},{7,3},{8,12},{9,13},{10,... | collective-permute-start | bytes 393224 | tf_op jit(solution)/shard_map/ppermute | solution.py:191
  80.2 7.8 %collective-permute-start.26 = (bf16[16,32,128]{2,1,0:T(8,128)(2,1)S(1)}, bf16[16,32,128]{2,1,0:T(8,128)(2,1)S(1)}, u32[]{:S(2)}, u32[]{:S(2)}) collective-permute-start(bf16[16,32,128]{2,1,0:T(8,128)(2,1)S(1)} %get-tuple-element.56.refs_3_), channel_id=1, source_target_pairs={{0,4},{1,5},{2,6},{3,7},{4,0},{5,1},{6,2},{7,3},{8,12},{9,13},{10,... | collective-permute-start | bytes 393224 | tf_op jit(solution)/shard_map/ppermute | solution.py:191
  85.3 3.9 %collective-permute-start.31 = (bf16[16,32,128]{2,1,0:T(8,128)(2,1)S(1)}, bf16[16,32,128]{2,1,0:T(8,128)(2,1)S(1)}, u32[]{:S(2)}, u32[]{:S(2)}) collective-permute-start(bf16[16,32,128]{2,1,0:T(8,128)(2,1)S(1)} %direct.5), channel_id=1, source_target_pairs={{0,2},{1,3},{2,0},{3,1},{4,6},{5,7},{6,4},{7,5},{8,10},{9,11},{10,... | collective-permute-start | bytes 393224 | tf_op jit(solution)/shard_map/ppermute | solution.py:191
  88.0 4.2 %collective-permute-start.27 = (bf16[16,32,128]{2,1,0:T(8,128)(2,1)S(1)}, bf16[16,32,128]{2,1,0:T(8,128)(2,1)S(1)}, u32[]{:S(2)}, u32[]{:S(2)}) collective-permute-start(bf16[16,32,128]{2,1,0:T(8,128)(2,1)S(1)} %add_convert_fusion), channel_id=1, source_target_pairs={{0,8},{1,9},{2,10},{3,11},{4,12},{5,13},{6,14},{7,15},{8,0},{9,1},... | collective-permute-start | bytes 393224 | tf_op jit(solution)/shard_map/ppermute | solution.py:191
  92.3 4.7 %collective-permute-start.32 = (bf16[8,32,128]{2,1,0:T(8,128)(2,1)S(1)}, bf16[8,32,128]{2,1,0:T(8,128)(2,1)S(1)}, u32[]{:S(2)}, u32[]{:S(2)}) collective-permute-start(bf16[8,32,128]{2,1,0:T(8,128)(2,1)S(1)} %slice.200), channel_id=1, source_target_pairs={{0,16},{1,17},{2,18},{3,19},{4,20},{5,21},{6,22},{7,23},{8,24},{9,... | collective-permute-start | bytes 196616 | tf_op jit(solution)/shard_map/ppermute | solution.py:191
  97.0 10.4 %collective-permute-start.34 = (f32[4,32,128]{2,1,0:T(8,128)S(1)}, f32[4,32,128]{2,1,0:T(8,128)S(1)}, u32[]{:S(2)}, u32[]{:S(2)}) collective-permute-start(f32[4,32,128]{2,1,0:T(8,128)S(1)} %get-tuple-element.81), channel_id=1, source_target_pairs={{1,0},{0,1},{17,2},{16,3},{5,4},{4,5},{21,6},{20,7},{9,8},{8,9},{2... | collective-permute-start | bytes 196616 | tf_op jit(solution)/shard_map/ppermute | solution.py:191
  104.7 8.0 %collective-permute-start.33 = (f32[4,32,128]{2,1,0:T(8,128)S(1)}, f32[4,32,128]{2,1,0:T(8,128)S(1)}, u32[]{:S(2)}, u32[]{:S(2)}) collective-permute-start(f32[4,32,128]{2,1,0:T(8,128)S(1)} %get-tuple-element.82), channel_id=1, source_target_pairs={{0,0},{1,1},{16,2},{17,3},{4,4},{5,5},{20,6},{21,7},{8,8},{9,9},{2... | collective-permute-start | bytes 196616 | tf_op jit(solution)/shard_map/ppermute | solution.py:191
